TPU v7x, 512 devices: a whole 4x4x16 slice. The times are simulated.
512 devices in a mesh: elem: 128 (over x, z, core), blk: 4 (over y).
Axes of the slice: x: 4, y: 4, z: 16, core: 2. Of those that a mesh axis runs over, the one named last changes fastest.
Arguments:
- diagonal_block_list: bfloat16 [512, 512, 512], P('elem', None, 'blk'), may hold values from -0.25 to 0.25
- neighbour_block_list: bfloat16 [512, 6, 512, 512], P('elem', None, None, 'blk'), may hold values from -0.25 to 0.25
- neighbours: int32 [512, 6], P('elem'), may hold values from 0 to 511, as said below
- damping: float32 [512, 512], P('elem', 'blk'), may hold values from 0.05 to 0.3
- bases: bfloat16 [512, 512, 128], P('elem', 'blk'), may hold values from -1.1953125 to 1.1953125
- agglomerate: int32 [512], replicated, may hold values from 0 to 255, as said below
- group: int32 [256], replicated, may hold values from 0 to 7
Outputs:
- smoothed: bfloat16 [512, 512, 128], P('elem', 'blk')
- coarse: float32 [256, 128, 128], P('elem', 'blk')
- last_level: float32 [8, 128, 128], P(None, 'blk')
Inputs may be any that keep to these rules, and one draw needn't show every extreme that they name: `neighbours`: each neighbour lies on the same index of elem as its element or on the next index on either side; every index of elem has a neighbour on an adjacent index. The elements of one agglomerate are consecutive; every agglomerate has one element or more.
All inputs are finite; a program needn't handle non-finite values.
Results may differ from a plain program's by a relative error of at most 0.007.
Values may be sent and summed in bfloat16 or wider, within the bound.
A program may use at most 64 MiB of HBM per device.

v0:
```python
import jax
import jax.numpy as jnp
from jax import lax
from jax.sharding import Mesh
from jax.sharding import PartitionSpec as P

SWEEPS = 2
NG = 8
ELEM = ("elem_0", "elem_1", "elem_2")


def extended(x, sides, width):
    for axis, dim in sides:
        size, length = (lax.axis_size(axis), x.shape[dim])
        up = [(i, (i + 1) % size) for i in range(size - 1)]
        down = [(j, i) for i, j in up]
        last = lax.slice_in_dim(x, length - width, length, axis=dim)
        initial = lax.slice_in_dim(x, 0, width, axis=dim)
        before = lax.ppermute(last, axis, up)
        after = lax.ppermute(initial, axis, down)
        x = jnp.concatenate([before, x, after], axis=dim)
    return x


def split_up(x, dim, length):
    dims = x.shape
    pieces = x.reshape(*dims[:dim], length, dims[dim] // length, *dims[dim + 1 :])
    return jnp.moveaxis(pieces, dim, 0)


def sent_and_summed(x, axis, dim):
    pieces = split_up(x, dim, lax.axis_size(axis))
    arrived = lax.all_to_all(pieces, axis, split_axis=0, concat_axis=0, tiled=True)
    return arrived.sum(axis=0)


def from_everyone(x, axis):
    copies = jnp.broadcast_to(x, (lax.axis_size(axis), *x.shape))
    return lax.all_to_all(copies, axis, split_axis=0, concat_axis=0, tiled=True)


def joined_along(pieces, dim):
    dims = list(pieces.shape[1:])
    dims[dim] *= pieces.shape[0]
    return jnp.moveaxis(pieces, 0, dim).reshape(dims)


def collect(x, axis, dim):
    pieces = from_everyone(x, axis)
    return joined_along(pieces, dim)


def summed_on_arrival(x, axis, dim):
    pieces = split_up(x, dim, lax.axis_size(axis))
    arrived = lax.all_to_all(pieces, axis, split_axis=0, concat_axis=0, tiled=True)
    return arrived.astype(jnp.float32).sum(axis=0)


def sent_together(arrays, axis, dim, along):
    ends, at = ([], 0)
    for a in arrays[:-1]:
        at += a.shape[along]
        ends.append(at)
    both = jnp.concatenate(arrays, axis=along)
    return tuple(jnp.split(summed_on_arrival(both, axis, dim), ends, axis=along))


def sum_by_axis(x, axes, dim):
    far, near = axes
    own = sent_and_summed(split_up(x, dim, lax.axis_size(far)), near, dim + 1)
    return jnp.sum(lax.all_to_all(own, far, 0, 0, tiled=True), axis=0)


def padded_to(lines, length):
    spare = -lines.shape[0] % length
    if not spare:
        return lines
    return jnp.concatenate([lines, jnp.zeros((spare, *lines.shape[1:]), lines.dtype)])


def gathered_by_axis(x, axes, dim):
    far, near = axes
    pieces = from_everyone(from_everyone(x, far), near)
    return joined_along(pieces.swapaxes(0, 1).reshape(-1, *x.shape), dim)


def sum_by_parts(x, axes):
    lines = x.reshape(-1, x.shape[-1])
    own = sum_by_axis(padded_to(lines, lax.axis_size(axes[0]) * lax.axis_size(axes[1])), axes, 0)
    whole = gathered_by_axis(own, axes, 0)
    return whole[: len(lines)].reshape(x.shape)


def nearby_slabs(slab, neighbour_ids, first_element):
    local_count = slab.shape[0]
    padded = extended(slab, ((ELEM, 0),), local_count)
    offsets = neighbour_ids - (first_element - local_count)
    return jnp.take(padded, offsets, axis=0)


def lookup_table(indices, table):
    positions = jnp.arange(table.shape[0], dtype=jnp.int32)
    matches = indices[..., None] == positions
    return jnp.sum(jnp.where(matches, table, 0), -1)


def body(diagonal_block_list, neighbour_block_list, neighbours, damping, bases, agglomerate, group):
    local_count = bases.shape[0]
    slab_rows = bases.shape[1]
    coarse_width = bases.shape[2]
    position = lax.axis_index(ELEM)
    first_element = position * local_count
    present_value = bases
    for sweep_index in range(SWEEPS):
        nearby_elements = nearby_slabs(present_value, neighbours, first_element)
        total_result = jnp.einsum(
            "dag,dgb->adb", diagonal_block_list, present_value, preferred_element_type=jnp.float32
        )
        total_result = total_result + jnp.einsum(
            "psgw,pswj->gpj",
            neighbour_block_list,
            nearby_elements,
            preferred_element_type=jnp.float32,
        )
        summed = sent_and_summed(
            total_result.reshape(slab_rows * lax.axis_size("blk"), local_count * coarse_width),
            "blk",
            0,
        )
        summed = summed.reshape(slab_rows, local_count, coarse_width).transpose(1, 0, 2)
        present_value = (present_value.astype(jnp.float32) - damping[:, :, None] * summed).astype(
            jnp.bfloat16
        )
    piece = collect(present_value, "blk", 1)
    diag_left = jnp.einsum(
        "eic,eis->ecs", piece, diagonal_block_list, preferred_element_type=jnp.float32
    )
    nbr_left = jnp.einsum(
        "eic,ekis->ekcs", piece, neighbour_block_list, preferred_element_type=jnp.float32
    )
    diag_left, nbr_left = (diag_left, nbr_left)
    diag_left = diag_left.astype(jnp.bfloat16)
    nbr_left = nbr_left.astype(jnp.bfloat16)
    nearby_elements = nearby_slabs(present_value, neighbours, first_element)
    self_terms = jnp.einsum(
        "ecs,esd->ecd", diag_left, present_value, preferred_element_type=jnp.float32
    )
    nbr_terms = jnp.einsum(
        "ekcs,eksd->ekcd", nbr_left, nearby_elements, preferred_element_type=jnp.float32
    )
    own_cluster = lax.dynamic_slice_in_dim(agglomerate, first_element, local_count)
    nbr_agg = lookup_table(neighbours, agglomerate)
    own_group = lookup_table(own_cluster, group)
    nbr_group = lookup_table(nbr_agg, group)
    same_cluster = (nbr_agg == own_cluster[:, None]).astype(jnp.float32)
    same_group = (nbr_group == own_group[:, None]).astype(jnp.float32)
    first_sum = self_terms + jnp.sum(same_cluster[:, :, None, None] * nbr_terms, 1)
    second_level_sum = self_terms + jnp.sum(same_group[:, :, None, None] * nbr_terms, 1)
    first_rows, second_rows = sent_together(
        (first_sum.astype(jnp.bfloat16), second_level_sum.astype(jnp.bfloat16)), "blk", 1, 0
    )
    owned_count = local_count // 2
    coarse_rows_count = first_rows.shape[1]
    owned_ids = position * owned_count + jnp.arange(owned_count, dtype=jnp.int32)
    empty_owned = jnp.zeros((owned_count, coarse_rows_count, coarse_width), jnp.float32)
    select = (agglomerate[:, None] == owned_ids[None, :]).astype(jnp.float32)
    coarse = empty_owned + jnp.einsum(
        "ra,rcd->acd",
        select,
        lax.all_gather(first_rows.astype(jnp.bfloat16), ELEM, axis=0, tiled=True).astype(
            jnp.float32
        ),
        precision=lax.Precision.HIGHEST,
    )
    group_select = (own_group[:, None] == jnp.arange(NG, dtype=jnp.int32)[None, :]).astype(
        jnp.float32
    )
    level_terms = jnp.einsum(
        "eg,ecd->gcd", group_select, second_rows, precision=lax.Precision.HIGHEST
    )
    last_level = sum_by_parts(level_terms, (("elem_0", "elem_1"), "elem_2"))
    return (present_value, coarse, last_level)


def solution(mesh):
    finer = Mesh(
        mesh.devices.reshape(4, 16, 2, mesh.shape["blk"]), ("elem_0", "elem_1", "elem_2", "blk")
    )
    return jax.shard_map(
        body,
        mesh=finer,
        in_specs=(
            P(ELEM, None, "blk"),
            P(ELEM, None, None, "blk"),
            P(ELEM, None),
            P(ELEM, "blk"),
            P(ELEM, "blk", None),
            P(),
            P(),
        ),
        out_specs=(P(ELEM, "blk", None), P(ELEM, "blk", None), P(None, "blk", None)),
        check_vma=False,
    )
```

profile of v0, /device:TPU:1, one launch (start us, length us, event | category | flops | bytes accessed | tf_op | source)
XLA Modules:
  0.0 289.4 jit_solution(1630384653250120855)
XLA Ops:
  7.2 5.2 %collective-permute-start = (bf16[4,128,128]{2,1,0:T(8,128)(2,1)}, bf16[4,128,128]{2,1,0:T(8,128)(2,1)S(1)}, u32[]{:S(2)}, u32[]{:S(2)}) collective-permute-start(bf16[4,128,128]{2,1,0:T(8,128)(2,1)} %param.13), channel_id=1, source_target_pairs={{0,4},{4,8},{8,12},{12,16},{16,20},{20,24},{24,28},{28,32},{32,36}... | collective-permute-start | bytes 393224 | tf_op jit(solution)/shard_map/ppermute | solution.py:19
  12.4 5.2 %collective-permute-start.1 = (bf16[4,128,128]{2,1,0:T(8,128)(2,1)}, bf16[4,128,128]{2,1,0:T(8,128)(2,1)}, u32[]{:S(2)}, u32[]{:S(2)}) collective-permute-start(bf16[4,128,128]{2,1,0:T(8,128)(2,1)} %param.13), channel_id=1, source_target_pairs={{4,0},{8,4},{12,8},{16,12},{20,16},{24,20},{28,24},{32,28},{36,32}... | collective-permute-start | bytes 393224 | tf_op jit(solution)/shard_map/ppermute | solution.py:20
  21.6 2.3 copy.88
  24.0 2.3 convolution_bitcast_fusion.1
  27.7 2.5 reshape_reshape.6
  30.2 2.3 copy.89
  32.6 4.2 %all-to-all-start = ((f32[4,128,512]{1,2,0:T(8,128)}), f32[4,128,512]{1,2,0:T(8,128)}, u32[]{:S(2)}, u32[]{:S(2)}) async-start(f32[4,128,512]{1,2,0:T(8,128)} %copy.89), calls=%async_computation | async-start | bytes 2097152 | tf_op jit(solution)/shard_map/all_to_all | solution.py:33
  37.0 15.0 %all-to-all-done = f32[4,128,512]{1,2,0:T(8,128)} async-done(((f32[4,128,512]{1,2,0:T(8,128)}), f32[4,128,512]{1,2,0:T(8,128)}, u32[]{:S(2)}, u32[]{:S(2)}) %all-to-all-start) | async-done | bytes 1048608 | tf_op jit(solution)/shard_map/all_to_all | solution.py:33
  53.3 2.9 %collective-permute-start.3 = (bf16[4,128,128]{1,2,0:T(8,128)(2,1)S(1)}, bf16[4,128,128]{1,2,0:T(8,128)(2,1)S(1)}, u32[]{:S(2)}, u32[]{:S(2)}) collective-permute-start(bf16[4,128,128]{1,2,0:T(8,128)(2,1)S(1)} %subtract_convert_fusion.1), channel_id=1, source_target_pairs={{4,0},{8,4},{12,8},{16,12},{20,16},{24,20},{28,24},{32,28},{36,32}... | collective-permute-start | bytes 393224 | tf_op jit(solution)/shard_map/ppermute | solution.py:20
  56.2 2.7 collective-permute-start.2
  62.4 2.3 convolution_bitcast_fusion
  66.1 2.6 reshape_reshape.7
  68.7 2.3 copy.90
  71.0 4.2 %all-to-all-start.1 = ((f32[4,128,512]{1,2,0:T(8,128)}), f32[4,128,512]{1,2,0:T(8,128)}, u32[]{:S(2)}, u32[]{:S(2)}) async-start(f32[4,128,512]{1,2,0:T(8,128)} %copy.90), calls=%async_computation.1 | async-start | bytes 2097152 | tf_op jit(solution)/shard_map/all_to_all | solution.py:33
  76.0 14.0 %all-to-all-done.1 = f32[4,128,512]{1,2,0:T(8,128)} async-done(((f32[4,128,512]{1,2,0:T(8,128)}), f32[4,128,512]{1,2,0:T(8,128)}, u32[]{:S(2)}, u32[]{:S(2)}) %all-to-all-start.1) | async-done | bytes 1048608 | tf_op jit(solution)/shard_map/all_to_all | solution.py:33
  90.0 2.0 reduce_sum.91
  94.0 4.1 %all-to-all-start.2 = ((bf16[4,4,128,128]{3,2,1,0:T(8,128)(2,1)}), bf16[4,4,128,128]{3,2,1,0:T(8,128)(2,1)}, u32[]{:S(2)}, u32[]{:S(2)}) async-start(bf16[4,4,128,128]{3,2,1,0:T(8,128)(2,1)} %broadcast_in_dim.58), calls=%async_computation.2 | async-start | bytes 1048576 | tf_op jit(solution)/shard_map/all_to_all | solution.py:39
  99.6 1.9 collective-permute-start.5
  101.5 4.2 %collective-permute-start.4 = (bf16[4,128,128]{1,2,0:T(8,128)(2,1)S(1)}, bf16[4,128,128]{1,2,0:T(8,128)(2,1)}, u32[]{:S(2)}, u32[]{:S(2)}) collective-permute-start(bf16[4,128,128]{1,2,0:T(8,128)(2,1)S(1)} %subtract_convert_fusion), channel_id=1, source_target_pairs={{0,4},{4,8},{8,12},{12,16},{16,20},{20,24},{24,28},{28,32},{32,36}... | collective-permute-start | bytes 393224 | tf_op jit(solution)/shard_map/ppermute | solution.py:19
  108.7 1.6 gather_fusion.2
  110.3 2.3 copy.98
  112.6 1.9 copy.92
  114.5 3.0 %multiply_reduce_fusion.1 = (f32[4,128,128]{2,1,0:T(8,128)}, f32[4,128,128]{2,1,0:T(8,128)}) fusion(f32[4,6]{1,0:T(4,128)S(1)} %copy-done.17, f32[4,6]{1,0:T(4,128)S(1)} %copy-done.18, bf16[4,6,128,128]{3,2,1,0:T(8,128)(2,1)} %copy.98, pred[4,6]{1,0:T(4,128)(4,1)S(1)} %get-tuple-element.24, bf16[4,512,128,1]{2,1,3,0:T(8,128)(2,1)} %bitcast.65, ...), kind=kOutput, calls=%fused_computation.6 | convolution fusion | flops 505544704 | bytes 4980952 | tf_op jit(solution)/shard_map/ekcs,eksd->ekcd/dot_general | solution.py:148
  117.6 1.8 add_convert_fusion.1
  119.4 10.7 %all_to_all.40 = bf16[4,8,32,128]{3,2,1,0:T(8,128)(2,1)S(1)} all-to-all(bf16[4,8,32,128]{3,2,1,0:T(8,128)(2,1)S(1)} %bitcast.70), channel_id=1, replica_groups=mesh['elem_0'=4,'elem_1'=16,'elem_2'=2,'blk'=4] {'blk'}, dimensions={0} | all-to-all | bytes 524288 | tf_op jit(solution)/shard_map/all_to_all | solution.py:55
  131.3 3.8 %all_to_all.41 = f32[2,64,2,128]{3,2,1,0:T(2,128)S(1)} all-to-all(f32[2,64,2,128]{3,2,1,0:T(2,128)S(1)} %copy.105), channel_id=1, replica_groups=mesh['elem_0'=4,'elem_1'=16,'elem_2'=2,'blk'=4] {'elem_2'}, dimensions={0} | all-to-all | bytes 262144 | tf_op jit(solution)/shard_map/all_to_all | solution.py:33
  135.2 34.8 %all_to_all.42 = f32[64,2,128]{2,1,0:T(2,128)S(1)} all-to-all(f32[64,2,128]{2,1,0:T(2,128)S(1)} %reduce_sum.98), channel_id=1, replica_groups=mesh['elem_0'=4,'elem_1'=16,'elem_2'=2,'blk'=4] {'elem_0','elem_1'}, dimensions={0} | all-to-all | bytes 131072 | tf_op jit(solution)/shard_map/all_to_all | solution.py:71
  170.7 5.7 %all-to-all-start.6 = ((f32[64,2,128]{2,1,0:T(2,128)}), f32[64,2,128]{2,1,0:T(2,128)S(1)}, u32[]{:S(2)}, u32[]{:S(2)}) async-start(f32[64,2,128]{2,1,0:T(2,128)} %broadcast_in_dim.65), calls=%async_computation.6 | async-start | bytes 131072 | tf_op jit(solution)/shard_map/all_to_all | solution.py:39
  176.4 13.5 %all-to-all-done.6 = f32[64,2,128]{2,1,0:T(2,128)S(1)} async-done(((f32[64,2,128]{2,1,0:T(2,128)}), f32[64,2,128]{2,1,0:T(2,128)S(1)}, u32[]{:S(2)}, u32[]{:S(2)}) %all-to-all-start.6) | async-done | bytes 65568 | tf_op jit(solution)/shard_map/all_to_all | solution.py:39
  190.0 5.6 %all_to_all.43 = f32[2,64,2,128]{3,2,1,0:T(2,128)S(1)} all-to-all(f32[2,64,2,128]{3,2,1,0:T(2,128)S(1)} %broadcast_in_dim.66), channel_id=1, replica_groups=mesh['elem_0'=4,'elem_1'=16,'elem_2'=2,'blk'=4] {'elem_2'}, dimensions={0} | all-to-all | bytes 262144 | tf_op jit(solution)/shard_map/all_to_all | solution.py:39
  196.3 82.2 %all-gather.2.cloned.1.call-done = bf16[512,32,128]{2,1,0:T(8,128)(2,1)} async-done(((bf16[4,32,128]{2,1,0:T(8,128)(2,1)}), bf16[512,32,128]{2,1,0:T(8,128)(2,1)}) %all-gather.2.cloned.1.call-update) | async-done | bytes 4194320 | tf_op jit(solution)/shard_map/all_gather | solution.py:170
  278.5 3.4 %fusion = f32[2,32,128]{2,0,1:T(2,128)S(1)} fusion(bf16[512,32,128]{2,1,0:T(8,128)(2,1)} %all-gather.2.cloned.1.call-done, s32[512]{0:T(512)S(1)} %copy-done.13, s32[2]{0:T(128)S(1)} %iota_add_fusion), kind=kOutput, calls=%fused_computation.3 | convolution fusion | flops 8389632 | bytes 4229128 | tf_op jit(solution)/shard_map/ra,rcd->acd/dot_general | solution.py:167
  (87 shorter events, 22.2 us)
Async XLA Ops:
  7.2 16.8 %copy-start = (bf16[4,6,512,128]{3,2,1,0:T(8,128)(2,1)S(1)}, bf16[4,6,512,128]{3,2,1,0:T(8,128)(2,1)}, u32[]{:S(2)}) copy-start(bf16[4,6,512,128]{3,2,1,0:T(8,128)(2,1)} %param.10) | copy-start | bytes 9437188
  7.2 11.2 %collective-permute-start = (bf16[4,128,128]{2,1,0:T(8,128)(2,1)}, bf16[4,128,128]{2,1,0:T(8,128)(2,1)S(1)}, u32[]{:S(2)}, u32[]{:S(2)}) collective-permute-start(bf16[4,128,128]{2,1,0:T(8,128)(2,1)} %param.13), channel_id=1, source_target_pairs={{0,4},{4,8},{8,12},{12,16},{16,20},{20,24},{24,28},{28,32},{32,36}... | collective-permute-start | bytes 393224 | tf_op jit(solution)/shard_map/ppermute | solution.py:19
  12.4 6.6 %collective-permute-start.1 = (bf16[4,128,128]{2,1,0:T(8,128)(2,1)}, bf16[4,128,128]{2,1,0:T(8,128)(2,1)}, u32[]{:S(2)}, u32[]{:S(2)}) collective-permute-start(bf16[4,128,128]{2,1,0:T(8,128)(2,1)} %param.13), channel_id=1, source_target_pairs={{4,0},{8,4},{12,8},{16,12},{20,16},{24,20},{28,24},{32,28},{36,32}... | collective-permute-start | bytes 393224 | tf_op jit(solution)/shard_map/ppermute | solution.py:20
  18.3 0.7 copy-start.9
  24.0 2.4 copy-start.1
  24.0 2.4 copy-start.7
  30.2 23.0 %copy-start.11 = (f32[4,128]{1,0:T(4,128)S(1)}, f32[4,128]{1,0:T(4,128)}, u32[]{:S(2)}) copy-start(f32[4,128]{1,0:T(4,128)} %param.12) | copy-start | bytes 6148
  32.6 19.4 %all-to-all-start = ((f32[4,128,512]{1,2,0:T(8,128)}), f32[4,128,512]{1,2,0:T(8,128)}, u32[]{:S(2)}, u32[]{:S(2)}) async-start(f32[4,128,512]{1,2,0:T(8,128)} %copy.89), calls=%async_computation | async-start | bytes 2097152 | tf_op jit(solution)/shard_map/all_to_all | solution.py:33
  53.3 7.5 %copy-start.5 = (bf16[4,128,128]{1,2,0:T(8,128)(2,1)}, bf16[4,128,128]{1,2,0:T(8,128)(2,1)S(1)}, u32[]{:S(2)}) copy-start(bf16[4,128,128]{1,2,0:T(8,128)(2,1)S(1)} %subtract_convert_fusion.1) | copy-start | bytes 393220
  53.3 6.3 %collective-permute-start.3 = (bf16[4,128,128]{1,2,0:T(8,128)(2,1)S(1)}, bf16[4,128,128]{1,2,0:T(8,128)(2,1)S(1)}, u32[]{:S(2)}, u32[]{:S(2)}) collective-permute-start(bf16[4,128,128]{1,2,0:T(8,128)(2,1)S(1)} %subtract_convert_fusion.1), channel_id=1, source_target_pairs={{4,0},{8,4},{12,8},{16,12},{20,16},{24,20},{28,24},{32,28},{36,32}... | collective-permute-start | bytes 393224 | tf_op jit(solution)/shard_map/ppermute | solution.py:20
  56.2 4.6 %collective-permute-start.2 = (bf16[4,128,128]{1,2,0:T(8,128)(2,1)S(1)}, bf16[4,128,128]{1,2,0:T(8,128)(2,1)S(1)}, u32[]{:S(2)}, u32[]{:S(2)}) collective-permute-start(bf16[4,128,128]{1,2,0:T(8,128)(2,1)S(1)} %subtract_convert_fusion.1), channel_id=1, source_target_pairs={{0,4},{4,8},{8,12},{12,16},{16,20},{20,24},{24,28},{28,32},{32,36}... | collective-permute-start | bytes 393224 | tf_op jit(solution)/shard_map/ppermute | solution.py:19
  62.4 2.4 copy-start.2
  62.4 2.4 copy-start.6
  66.1 9.1 %copy-start.14 = (s32[4,6]{1,0:T(4,128)S(1)}, s32[4,6]{1,0:T(4,128)}, u32[]{:S(2)}) copy-start(s32[4,6]{1,0:T(4,128)} %param.11) | copy-start | bytes 292
  66.1 9.2 %copy-start.12 = (s32[512]{0:T(512)S(1)}, s32[512]{0:T(512)}, u32[]{:S(2)}) copy-start(s32[512]{0:T(512)} %param.14) | copy-start | bytes 6148
  66.1 9.6 %copy-start.16 = (s32[256]{0:T(256)S(1)}, s32[256]{0:T(256)}, u32[]{:S(2)}) copy-start(s32[256]{0:T(256)} %param.15) | copy-start | bytes 3076
  71.0 18.9 %all-to-all-start.1 = ((f32[4,128,512]{1,2,0:T(8,128)}), f32[4,128,512]{1,2,0:T(8,128)}, u32[]{:S(2)}, u32[]{:S(2)}) async-start(f32[4,128,512]{1,2,0:T(8,128)} %copy.90), calls=%async_computation.1 | async-start | bytes 2097152 | tf_op jit(solution)/shard_map/all_to_all | solution.py:33
  93.0 14.0 %copy-start.3 = (bf16[4,128,128]{1,2,0:T(8,128)(2,1)}, bf16[4,128,128]{1,2,0:T(8,128)(2,1)S(1)}, u32[]{:S(2)}) copy-start(bf16[4,128,128]{1,2,0:T(8,128)(2,1)S(1)} %subtract_convert_fusion) | copy-start | bytes 393220
  93.1 13.9 %copy-start.8 = (bf16[4,128,128]{2,1,0:T(8,128)(2,1)}, bf16[4,128,128]{2,1,0:T(8,128)(2,1)S(1)}, u32[]{:S(2)}) copy-start(bf16[4,128,128]{2,1,0:T(8,128)(2,1)S(1)} %copy.108) | copy-start | bytes 393220
  94.0 18.6 %all-to-all-start.2 = ((bf16[4,4,128,128]{3,2,1,0:T(8,128)(2,1)}), bf16[4,4,128,128]{3,2,1,0:T(8,128)(2,1)}, u32[]{:S(2)}, u32[]{:S(2)}) async-start(bf16[4,4,128,128]{3,2,1,0:T(8,128)(2,1)} %broadcast_in_dim.58), calls=%async_computation.2 | async-start | bytes 1048576 | tf_op jit(solution)/shard_map/all_to_all | solution.py:39
  98.2 180.3 %all-gather.2.cloned.1.call-start = ((), (), s32[]{:S(2)}) async-start(), calls=%async_computation.8 | async-start | bytes 4227072 | tf_op jit(solution)/shard_map/all_gather | solution.py:170
  99.6 7.4 %collective-permute-start.5 = (bf16[4,128,128]{1,2,0:T(8,128)(2,1)S(1)}, bf16[4,128,128]{1,2,0:T(8,128)(2,1)S(1)}, u32[]{:S(2)}, u32[]{:S(2)}) collective-permute-start(bf16[4,128,128]{1,2,0:T(8,128)(2,1)S(1)} %subtract_convert_fusion), channel_id=1, source_target_pairs={{4,0},{8,4},{12,8},{16,12},{20,16},{24,20},{28,24},{32,28},{36,32}... | collective-permute-start | bytes 393224 | tf_op jit(solution)/shard_map/ppermute | solution.py:20
  101.5 6.1 %collective-permute-start.4 = (bf16[4,128,128]{1,2,0:T(8,128)(2,1)S(1)}, bf16[4,128,128]{1,2,0:T(8,128)(2,1)}, u32[]{:S(2)}, u32[]{:S(2)}) collective-permute-start(bf16[4,128,128]{1,2,0:T(8,128)(2,1)S(1)} %subtract_convert_fusion), channel_id=1, source_target_pairs={{0,4},{4,8},{8,12},{12,16},{16,20},{20,24},{24,28},{28,32},{32,36}... | collective-permute-start | bytes 393224 | tf_op jit(solution)/shard_map/ppermute | solution.py:19
  106.3 8.2 %copy-start.17 = (f32[4,6]{1,0:T(4,128)S(1)}, f32[4,6]{1,0:T(4,128)}, u32[]{:S(2)}) copy-start(f32[4,6]{1,0:T(4,128)} %copy.96) | copy-start | bytes 292
  107.0 7.5 %copy-start.18 = (f32[4,6]{1,0:T(4,128)S(1)}, f32[4,6]{1,0:T(4,128)}, u32[]{:S(2)}) copy-start(f32[4,6]{1,0:T(4,128)} %copy.99) | copy-start | bytes 292
  107.0 0.7 copy-start.10
  114.5 3.1 %copy-start.4 = (bf16[4,128,128]{1,2,0:T(8,128)(2,1)S(1)}, bf16[4,128,128]{1,2,0:T(8,128)(2,1)}, u32[]{:S(2)}) copy-start(bf16[4,128,128]{1,2,0:T(8,128)(2,1)} %copy-done.3) | copy-start | bytes 393220
  117.5 13.3 %copy-start.15 = (s32[4]{0:T(128)S(1)}, s32[4]{0:T(128)}, u32[]{:S(2)}) copy-start(s32[4]{0:T(128)} %select_reduce_fusion.2) | copy-start | bytes 52
  117.6 161.0 %copy-start.13 = (s32[512]{0:T(512)S(1)}, s32[512]{0:T(512)}, u32[]{:S(2)}) copy-start(s32[512]{0:T(512)} %param.14) | copy-start | bytes 6148
  170.7 19.2 %all-to-all-start.6 = ((f32[64,2,128]{2,1,0:T(2,128)}), f32[64,2,128]{2,1,0:T(2,128)S(1)}, u32[]{:S(2)}, u32[]{:S(2)}) async-start(f32[64,2,128]{2,1,0:T(2,128)} %broadcast_in_dim.65), calls=%async_computation.6 | async-start | bytes 131072 | tf_op jit(solution)/shard_map/all_to_all | solution.py:39
Sparse Core Ops, SparseCore 0:
  131.0 147.4 all-gather.1
where the time goes:
time: 291 us; the launch traced here: 289 us
  waiting for transfers between devices  127 us (44%)
  blocking collectives  55 us (19%)
  starting transfers between devices  40.4 us (14%)
  local copies, waits for them, and re-layouts  27.8 us (10%)
  matrix products  16 us (5%)
  between operations  14.4 us (5%)
  other arithmetic  9.23 us (3%)
    all_gather x1, waiting for transfers between devices, body(): lax.all_gather(first_rows.astype(jnp.bfloat16), ELEM, axis=0, tiled=True)  82.2 us
    all_to_all x1, blocking collectives, sum_by_axis(): return jnp.sum(lax.all_to_all(own, far, 0, 0, tiled=True), axis=0)  34.8 us
    all_to_all x2, waiting for transfers between devices, sent_and_summed(): lax.all_to_all(pieces, axis, split_axis=0, concat_axis=0, tiled=True)  29 us
    all_to_all x2, waiting for transfers between devices, from_everyone(): return lax.all_to_all(copies, axis, split_axis=0, concat_axis=0, tiled=True)  13.5 us
    ppermute x3, starting transfers between devices, extended(): before = lax.ppermute(last, axis, up)  12 us
    all_to_all x1, blocking collectives, summed_on_arrival(): lax.all_to_all(pieces, axis, split_axis=0, concat_axis=0, tiled=True)  10.7 us
    ppermute x3, starting transfers between devices, extended(): after = lax.ppermute(initial, axis, down)  9.97 us
    all_to_all x2, starting transfers between devices, from_everyone(): return lax.all_to_all(copies, axis, split_axis=0, concat_axis=0, tiled=True)  9.82 us
  transfers between devices with their start and end apart: 11, of which 6 were waited for; matrix products, arithmetic and copies ran while one was open for 4% of the time, Pallas kernels for 0%

commit v1 on v0

v1 whole, which is shorter than its diff:
```python
import functools

import jax
import jax.numpy as jnp
from jax import lax
from jax.experimental import pallas as pl
from jax.experimental.pallas import tpu as pltpu
from jax.sharding import PartitionSpec as P

MESH = pl.DeviceIdType.MESH
F32 = jnp.float32
BF16 = jnp.bfloat16
NL = 4
NBR = 6
BLK = 4
NX = 4
NC = 128
RB = 128
ROWS = RB * BLK
KK = (NBR + 1) * RB
HR = NC // BLK
SWEEPS = 2


def remote(src, dst, send_sem, recv_sem, device):
    return pltpu.make_async_remote_copy(
        src_ref=src,
        dst_ref=dst,
        send_sem=send_sem,
        recv_sem=recv_sem,
        device_id=device,
        device_id_type=MESH,
    )


def kernel(
    nz,
    nbr_s,
    agg_s,
    grp_s,
    damp_ref,
    diag_hbm,
    nbrs_hbm,
    bases_hbm,
    smooth_ref,
    coarse_ref,
    last_ref,
    a_v,
    xe0,
    xe1,
    xe2,
    xg,
    xg2,
    dmp,
    ysum,
    y_opp,
    y_plain,
    y_relay,
    y_r1,
    y_rp,
    y_rr,
    xa,
    zs,
    gsum,
    g_opp,
    g_plain,
    g_relay,
    g_r1,
    g_rp,
    g_rr,
    gx,
    c8h,
    hs,
    hx,
    km,
    pb,
    rz,
    l1,
    l2,
    ll,
    a_sem,
    b_sem,
    halo_ss,
    halo_rs,
    y_ss,
    y_rs,
    ag_ss,
    ag_rs,
    d_ss,
    d_rs,
    x_ss,
    x_rs,
    z_ss,
    z_rs,
    l1_ss,
    l1_rs,
    l2_ss,
    l2_rs,
    f_ss,
    f_rs,
):
    xe = (xe0, xe1, xe2)
    ne = nz * NX * 2
    zl_n = min(4, nz)
    zh_n = nz // zl_n
    me = lax.axis_index("elem")
    b = lax.axis_index("blk")
    core = lax.rem(me, 2)
    zc = lax.rem(me // 2, nz)
    xc = me // (2 * nz)
    rt = lax.rem(b + 1, BLK)
    op = lax.rem(b + 2, BLK)
    lt = lax.rem(b + 3, BLK)
    nxt = (lax.rem(me + 1, ne), b)
    prv = (lax.rem(me + ne - 1, ne), b)
    right, left = (me, rt), (me, lt)

    def at(x, z, c):
        return ((x * nz + z) * 2 + c, b)

    line = []
    for dx in range(NX):
        for dc in range(2):
            if dx or dc:
                line.append(at(lax.rem(xc + dx, NX), zc, lax.rem(core + dc, 2)))

    barrier = pltpu.get_barrier_semaphore()
    partners = [nxt, prv, right, left, *line]
    for dev in partners:
        pl.semaphore_signal(barrier, inc=1, device_id=dev, device_id_type=MESH)

    def greet(dz, carry):
        pl.semaphore_signal(
            barrier,
            inc=1,
            device_id=at(xc, lax.rem(zc + dz, nz), core),
            device_id_type=MESH,
        )
        return carry

    lax.fori_loop(1, nz, greet, 0)

    own_in = pltpu.make_async_copy(bases_hbm, xe[0].at[pl.ds(NL, NL)], b_sem)
    own_in.start()

    def load_a(e, carry):
        pltpu.make_async_copy(
            diag_hbm.at[e], a_v.at[e, :, pl.ds(0, RB)], a_sem.at[e]
        ).start()
        for k in range(NBR):
            pltpu.make_async_copy(
                nbrs_hbm.at[e, k],
                a_v.at[e, :, pl.ds((k + 1) * RB, RB)],
                a_sem.at[e],
            ).start()
        return carry

    lax.fori_loop(0, NL, load_a, 0)

    pl.semaphore_wait(barrier, len(partners) + nz - 1)

    h0n = remote(bases_hbm, xe[0].at[pl.ds(0, NL)], halo_ss.at[0, 0, 0], halo_rs.at[0, 0, 0], nxt)
    h0p = remote(
        bases_hbm, xe[0].at[pl.ds(2 * NL, NL)], halo_ss.at[0, 1, 0], halo_rs.at[0, 1, 0], prv
    )
    h0n.start()
    h0p.start()

    for e in range(NL):
        dmp[e] = jnp.broadcast_to(damp_ref[pl.ds(e, 1), :], (RB, NC)).T

    lane = lax.broadcasted_iota(jnp.int32, (16, 512), 1)
    row = lax.broadcasted_iota(jnp.int32, (16, 512), 0)

    def place(i, slots):
        xx, cc, j = i // 8, lax.rem(i // 4, 2), lax.rem(i, 4)
        a = agg_s[((xx * nz + zc) * 2 + cc) * NL + j]
        dev = a // 2
        mine = (lax.rem(dev, 2) == core) & (dev // (2 * nz) == xc)
        slot = jnp.where(mine, lax.rem(dev // 2, nz) * 2 + lax.rem(a, 2), -1)
        return jnp.where(lane // 16 == i, slot, slots)

    slots = lax.fori_loop(0, 32, place, jnp.full((16, 512), -1, jnp.int32))
    same_row = row == lax.rem(lane, 16)

    def fill(s, carry):
        km[pl.ds(pl.multiple_of(s * 16, 16), 16), :] = jnp.where(
            (slots == s) & same_row, 1.0, 0.0
        ).astype(BF16)
        return carry

    lax.fori_loop(0, 2 * nz, fill, 0)

    own_in.wait()
    h0n.wait_recv()
    h0p.wait_recv()

    first = (me - 1) * NL

    def nearby(e, k):
        return jnp.clip(nbr_s[e, k] - first, 0, 3 * NL - 1)

    def wait_a(e):
        pltpu.make_async_copy(a_v.at[e], a_v.at[e], a_sem.at[e]).wait()

    def sides(to_right):
        if to_right:
            return right, rt, left, lt
        return left, lt, right, rt

    def opp_copy(st, e, bufs, to_right):
        near = sides(to_right)[0]
        return remote(bufs[1].at[e], bufs[4].at[e], y_ss.at[st, 0, e], y_rs.at[st, 0, e], near)

    def plain_copy(st, e, bufs, to_right):
        far = sides(to_right)[2]
        return remote(bufs[2].at[e], bufs[5].at[e], y_ss.at[st, 1, e], y_rs.at[st, 1, e], far)

    def relay_copy(st, e, bufs, to_right):
        near = sides(to_right)[0]
        return remote(bufs[3].at[e], bufs[6].at[e], y_ss.at[st, 2, e], y_rs.at[st, 2, e], near)

    def reduce_send(st, e, bufs, to_right):
        total, opp, plain = bufs[:3]
        opp[e] = total[e, op].astype(BF16)
        opp_copy(st, e, bufs, to_right).start()
        plain[e] = total[e, sides(to_right)[3]].astype(BF16)
        plain_copy(st, e, bufs, to_right).start()

    def reduce_relay(st, e, bufs, to_right):
        opp_copy(st, e, bufs, to_right).wait_recv()
        bufs[3][e] = (bufs[0][e, sides(to_right)[1]] + bufs[4][e].astype(F32)).astype(BF16)
        relay_copy(st, e, bufs, to_right).start()

    def reduced(st, e, bufs, to_right):
        plain_copy(st, e, bufs, to_right).wait_recv()
        relay_copy(st, e, bufs, to_right).wait_recv()
        return bufs[0][e, b] + bufs[5][e].astype(F32) + bufs[6][e].astype(F32)

    def reduce_drain(st, bufs):
        def drain(i, carry):
            for e, to_right in ((i, True), (i + 2, False)):
                opp_copy(st, e, bufs, to_right).wait_send()
                plain_copy(st, e, bufs, to_right).wait_send()
                relay_copy(st, e, bufs, to_right).wait_send()
            return carry

        lax.fori_loop(0, 2, drain, 0)

    def pairs(step):
        def one(i, carry):
            step(i, True)
            step(i + 2, False)
            return carry

        lax.fori_loop(0, 2, one, 0)

    def halo_next(st, e):
        return remote(
            xe[st].at[NL + e], xe[st].at[e], halo_ss.at[st, 0, e], halo_rs.at[st, 0, e], nxt
        )

    def halo_prev(st, e):
        return remote(
            xe[st].at[NL + e], xe[st].at[2 * NL + e], halo_ss.at[st, 1, e], halo_rs.at[st, 1, e], prv
        )

    def gather_right(e, owner):
        return remote(
            xe[SWEEPS].at[NL + e], xa.at[e, owner], ag_ss.at[0, e], ag_rs.at[0, e], right
        )

    def gather_left(e, owner):
        return remote(
            xe[SWEEPS].at[NL + e], xa.at[e, owner], ag_ss.at[1, e], ag_rs.at[1, e], left
        )

    def gather_on(e, to_right, owner):
        near = sides(to_right)[0]
        return remote(xa.at[e, owner], xa.at[e, owner], ag_ss.at[2, e], ag_rs.at[2, e], near)

    for s in range(SWEEPS):
        bufs = (
            ysum,
            y_opp.at[s],
            y_plain.at[s],
            y_relay.at[s],
            y_r1.at[s],
            y_rp.at[s],
            y_rr.at[s],
        )

        def product(e, to_right, s=s, bufs=bufs):
            if s == 0:
                wait_a(e)
            xg[pl.ds(0, RB), :] = xe[s][NL + e]
            for k in range(NBR):
                xg[pl.ds((k + 1) * RB, RB), :] = xe[s][nearby(e, k)]
            y = jnp.dot(a_v[e], xg[...], preferred_element_type=F32)
            ysum[e] = y.reshape(BLK, RB, NC)
            reduce_send(s, e, bufs, to_right)

        pairs(product)
        pairs(functools.partial(lambda e, to_right, s, bufs: reduce_relay(s, e, bufs, to_right), s=s, bufs=bufs))

        def update(e, to_right, s=s, bufs=bufs):
            y = reduced(s, e, bufs, to_right)
            new = (xe[s][NL + e].astype(F32) - dmp[e] * y).astype(BF16)
            xe[s + 1][NL + e] = new
            halo_next(s + 1, e).start()
            halo_prev(s + 1, e).start()
            if s == SWEEPS - 1:
                gather_right(e, b).start()
                gather_left(e, b).start()
                smooth_ref[e] = new
                xa[e, b] = new

        pairs(update)

        def halo_in(e, carry, s=s):
            halo_next(s + 1, e).wait_recv()
            halo_prev(s + 1, e).wait_recv()
            return carry

        lax.fori_loop(0, NL, halo_in, 0)

    def forward(e, to_right):
        if to_right:
            gather_right(e, lt).wait_recv()
            gather_on(e, True, lt).start()
        else:
            gather_left(e, rt).wait_recv()
            gather_on(e, False, rt).start()

    pairs(forward)

    def couple(e, carry):
        own = me * NL + e
        own_agg = agg_s[own]
        own_grp = grp_s[own_agg]
        x_own = xe[SWEEPS][NL + e]
        xg2[pl.ds(0, RB), pl.ds(0, NC)] = x_own
        xg2[pl.ds(0, RB), pl.ds(NC, NC)] = x_own
        for k in range(NBR):
            near_agg = agg_s[nbr_s[e, k]]
            near_grp = grp_s[near_agg]
            x_near = xe[SWEEPS][nearby(e, k)].astype(F32)
            in_agg = jnp.where(near_agg == own_agg, 1.0, 0.0).astype(F32)
            in_grp = jnp.where(near_grp == own_grp, 1.0, 0.0).astype(F32)
            xg2[pl.ds((k + 1) * RB, RB), pl.ds(0, NC)] = (x_near * in_agg).astype(BF16)
            xg2[pl.ds((k + 1) * RB, RB), pl.ds(NC, NC)] = (x_near * in_grp).astype(BF16)
        zs[e] = jnp.dot(a_v[e], xg2[...], preferred_element_type=F32).astype(BF16)
        return carry

    lax.fori_loop(0, NL, couple, 0)

    gbufs = (gsum, g_opp, g_plain, g_relay, g_r1, g_rp, g_rr)

    def contract(e, to_right):
        if to_right:
            gather_left(e, rt).wait_recv()
        else:
            gather_right(e, lt).wait_recv()
        gather_on(e, to_right, op).wait_recv()
        both = lax.dot_general(
            xa[e].reshape(ROWS, NC), zs[e], (((0,), (0,)), ((), ())), preferred_element_type=F32
        )
        gsum[e] = both.reshape(BLK, HR, 2 * NC)
        reduce_send(SWEEPS, e, gbufs, to_right)

    pairs(contract)
    pairs(lambda e, to_right: reduce_relay(SWEEPS, e, gbufs, to_right))

    def settle(e, to_right):
        both = reduced(SWEEPS, e, gbufs, to_right).astype(BF16)
        gx[xc, core * NL + e] = both[:, :NC]
        c8h[core * NL + e] = both[:, NC:]

    pairs(settle)

    mate = at(xc, zc, 1 - core)
    here = pl.ds(core * NL, NL)
    there = pl.ds((1 - core) * NL, NL)

    def mate_copies(span):
        return (
            remote(gx.at[xc, span], gx.at[xc, span], d_ss.at[0], d_rs.at[0], mate),
            remote(c8h.at[span], c8h.at[span], d_ss.at[1], d_rs.at[1], mate),
        )

    for copy in mate_copies(here):
        copy.start()
    for copy in mate_copies(there):
        copy.wait_recv()

    def x_copies(dx, owner):
        to = lax.rem(xc + dx, NX)
        dev = at(to, zc, core)
        return (
            remote(gx.at[owner], gx.at[owner], x_ss.at[dx - 1, 0], x_rs.at[dx - 1, 0], dev),
            remote(hs.at[to], hx.at[owner], x_ss.at[dx - 1, 1], x_rs.at[dx - 1, 1], dev),
        )

    for dx in range(1, NX):
        x_copies(dx, xc)[0].start()
    for dx in range(NX):
        to = lax.rem(xc + dx, NX)
        acc = jnp.zeros((HR, NC), F32)
        for i in range(2 * NL):
            g = grp_s[agg_s[(me // 2) * (2 * NL) + i]]
            acc = acc + jnp.where(g == 2 * to + core, 1.0, 0.0).astype(F32) * c8h[i].astype(F32)
        if dx:
            hs[to] = acc.astype(BF16)
            x_copies(dx, xc)[1].start()
        else:
            hx[xc] = acc.astype(BF16)
    for dx in range(1, NX):
        for copy in x_copies(dx, lax.rem(xc + NX - dx, NX)):
            copy.wait_recv()

    zh, zl = zc // zl_n, lax.rem(zc, zl_n)

    def l1_copy(d, owner):
        dev = at(xc, zh * zl_n + lax.rem(zl + d, zl_n), core)
        return remote(l1.at[owner], l1.at[owner], l1_ss.at[d - 1], l1_rs.at[d - 1], dev)

    def l2_copy(d, owner):
        dev = at(xc, lax.rem(zh + d, zh_n) * zl_n + zl, core)
        return remote(l2.at[owner], l2.at[owner], l2_ss.at[d - 1], l2_rs.at[d - 1], dev)

    def summed(ref, n):
        acc = ref[0].astype(F32)
        for i in range(1, n):
            acc = acc + ref[i].astype(F32)
        return acc

    l1[zl] = summed(hx, NX).astype(BF16)
    for d in range(1, zl_n):
        l1_copy(d, zl).start()

    for h in range(HR // 16):
        part = gx[:, :, h * 16 : (h + 1) * 16, :].reshape(512, NC)
        sums = jnp.dot(km[...], part, preferred_element_type=F32)
        pb[:, h * 16 : (h + 1) * 16, :] = sums.reshape(2 * nz, 16, NC).astype(BF16)

    def z_copy(dz):
        to = lax.rem(zc + dz, nz)
        return remote(
            pb.at[pl.ds(to * 2, 2)], rz.at[dz], z_ss.at[dz - 1], z_rs.at[dz - 1], at(xc, to, core)
        )

    def z_start(dz, carry):
        z_copy(dz).start()
        return carry

    lax.fori_loop(1, nz, z_start, 0)

    for d in range(1, zl_n):
        l1_copy(d, lax.rem(zl + zl_n - d, zl_n)).wait_recv()
    l2[zh] = summed(l1, zl_n).astype(BF16)
    for d in range(1, zh_n):
        l2_copy(d, zh).start()
    for d in range(1, zh_n):
        l2_copy(d, lax.rem(zh + zh_n - d, zh_n)).wait_recv()
    mine = 2 * xc + core
    ll[mine] = summed(l2, zh_n)

    def final_copy(i, owner):
        return remote(ll.at[owner], ll.at[owner], f_ss.at[i], f_rs.at[i], line[i])

    for i in range(len(line)):
        final_copy(i, mine).start()

    def z_sum(dz, acc):
        z_copy(dz).wait_recv()
        return acc + rz[dz].astype(F32)

    coarse_ref[...] = lax.fori_loop(1, nz, z_sum, pb[pl.ds(zc * 2, 2)].astype(F32))

    i = 0
    for dx in range(NX):
        for dc in range(2):
            if dx or dc:
                owner = 2 * lax.rem(xc + NX - dx, NX) + lax.rem(core + dc, 2)
                final_copy(i, owner).wait_recv()
                i += 1
    last_ref[...] = ll[...]

    h0n.wait_send()
    h0p.wait_send()

    def halo_out(e, carry):
        for s in range(SWEEPS):
            halo_next(s + 1, e).wait_send()
            halo_prev(s + 1, e).wait_send()
        gather_right(e, b).wait_send()
        gather_left(e, b).wait_send()
        return carry

    lax.fori_loop(0, NL, halo_out, 0)
    pairs(lambda e, to_right: gather_on(e, to_right, lt if to_right else rt).wait_send())
    for s in range(SWEEPS):
        reduce_drain(
            s,
            (ysum, y_opp.at[s], y_plain.at[s], y_relay.at[s], y_r1.at[s], y_rp.at[s], y_rr.at[s]),
        )
    reduce_drain(SWEEPS, gbufs)
    for copy in mate_copies(here):
        copy.wait_send()
    for dx in range(1, NX):
        for copy in x_copies(dx, xc):
            copy.wait_send()
    for d in range(1, zl_n):
        l1_copy(d, zl).wait_send()
    for d in range(1, zh_n):
        l2_copy(d, zh).wait_send()
    for i in range(len(line)):
        final_copy(i, mine).wait_send()

    def z_out(dz, carry):
        z_copy(dz).wait_send()
        return carry

    lax.fori_loop(1, nz, z_out, 0)


def body(nz, diag, nbrs, neighbours, damping, bases, agglomerate, group):
    vmem = pl.BlockSpec(memory_space=pltpu.VMEM)
    smem = pl.BlockSpec(memory_space=pltpu.SMEM)
    hbm = pl.BlockSpec(memory_space=pltpu.HBM)
    zl_n = min(4, nz)
    dma = pltpu.SemaphoreType.DMA
    V = pltpu.VMEM
    el = (NL, RB, NC)
    gel = (NL, HR, 2 * NC)
    scratch = [
        V((NL, ROWS, KK), BF16),
        *[V((3 * NL, RB, NC), BF16) for _ in range(SWEEPS + 1)],
        V((KK, NC), BF16),
        V((KK, 2 * NC), BF16),
        V((NL, RB, NC), F32),
        V((NL, BLK, RB, NC), F32),
        *[V((SWEEPS, *el), BF16) for _ in range(6)],
        V((NL, BLK, RB, NC), BF16),
        V((NL, ROWS, 2 * NC), BF16),
        V((NL, BLK, HR, 2 * NC), F32),
        *[V(gel, BF16) for _ in range(6)],
        V((NX, 2 * NL, HR, NC), BF16),
        V((2 * NL, HR, NC), BF16),
        V((NX, HR, NC), BF16),
        V((NX, HR, NC), BF16),
        V((2 * nz * 16, 512), BF16),
        V((2 * nz, HR, NC), BF16),
        V((nz, 2, HR, NC), BF16),
        V((zl_n, HR, NC), BF16),
        V((nz // zl_n, HR, NC), BF16),
        V((8, HR, NC), F32),
        dma((NL,)),
        dma,
        dma((SWEEPS + 1, 2, NL)),
        dma((SWEEPS + 1, 2, NL)),
        dma((SWEEPS + 1, 3, NL)),
        dma((SWEEPS + 1, 3, NL)),
        dma((3, NL)),
        dma((3, NL)),
        dma((2,)),
        dma((2,)),
        dma((NX - 1, 2)),
        dma((NX - 1, 2)),
        dma((nz - 1,)),
        dma((nz - 1,)),
        dma((3,)),
        dma((3,)),
        dma((3,)),
        dma((3,)),
        dma((2 * NX - 1,)),
        dma((2 * NX - 1,)),
    ]
    return pl.pallas_call(
        functools.partial(kernel, nz),
        out_shape=(
            jax.ShapeDtypeStruct((NL, RB, NC), BF16),
            jax.ShapeDtypeStruct((2, HR, NC), F32),
            jax.ShapeDtypeStruct((8, HR, NC), F32),
        ),
        in_specs=[smem, smem, smem, vmem, hbm, hbm, hbm],
        out_specs=(vmem, vmem, vmem),
        scratch_shapes=scratch,
        compiler_params=pltpu.CompilerParams(
            collective_id=0, has_side_effects=True, vmem_limit_bytes=48 * 1024 * 1024
        ),
        name="galerkin",
    )(neighbours, agglomerate, group, damping, diag, nbrs, bases)


def solution(mesh):
    nz = mesh.shape["elem"] // (2 * NX)
    return jax.shard_map(
        functools.partial(body, nz),
        mesh=mesh,
        in_specs=(
            P("elem", None, "blk"),
            P("elem", None, None, "blk"),
            P("elem", None),
            P("elem", "blk"),
            P("elem", "blk", None),
            P(),
            P(),
        ),
        out_specs=(P("elem", "blk", None), P("elem", "blk", None), P(None, "blk", None)),
        check_vma=False,
    )
```

time: 291 us -> 95.2 us (0.33)
  waiting for transfers between devices: 127 us -> 0 us
  Pallas kernels: 0 us -> 85.8 us
  blocking collectives: 55 us -> 0 us
  starting transfers between devices: 40.4 us -> 0 us
  local copies, waits for them, and re-layouts: 27.8 us -> 8.48 us
  matrix products: 16 us -> 0 us
  between operations: 14.4 us -> 0.66 us
  other arithmetic: 9.23 us -> 0 us
    pallas_call x0 -> x1, Pallas kernels: none -> 85.8 us  [body(): pl.pallas_call(functools.partial(kernel, nz), out_shape=(jax.ShapeDtypeSt...]
    all_gather x1 -> x0, waiting for transfers between devices: 82.2 us -> none  [body(): lax.all_gather(first_rows.astype(jnp.bfloat16), ELEM, axis=0, tiled=True)]
    all_to_all x4 -> x0, blocking collectives: 55 us -> none  [the longest x1 34.8 us: sum_by_axis(): return jnp.sum(lax.all_to_all(own, far, 0, 0, tiled=True), axis=0)]
    all_to_all x4 -> x0, waiting for transfers between devices: 42.5 us -> none  [the longest x2 29 us: sent_and_summed(): lax.all_to_all(pieces, axis, split_axis=0, concat_axis=0, tiled=True)]
    ppermute x6 -> x0, starting transfers between devices: 22 us -> none  [the longest x3 12 us: extended(): before = lax.ppermute(last, axis, up)]
    all_to_all x4 -> x0, starting transfers between devices: 18.3 us -> none  [the longest x2 9.82 us: from_everyone(): return lax.all_to_all(copies, axis, split_axis=0, concat_axis=0, tiled=True)]
    dot_general x8 -> x0, matrix products: 16 us -> none  [the longest x2 4.69 us: body(): jnp.einsum('psgw,pswj->gpj', neighbour_block_list, nearby_elements, prefe...]
    another operation x4 -> x0, local copies, waits for them, and re-layouts: 9.73 us -> none  [split_up(): x.reshape(*dims[:dim], length, dims[dim] // length, *dims[dim + 1:])]
  transfers between devices with their start and end apart: 11 -> 0, of which waited for: 6 -> 0; matrix products, arithmetic and copies ran while one was open for 4% -> 0% of each run, Pallas kernels for 0% -> 0%
where the time goes in v1:
time: 95.2 us; the launch traced here: 94.9 us
  Pallas kernels  85.8 us (90%)
  local copies, waits for them, and re-layouts  8.48 us (9%)
    pallas_call x1, Pallas kernels, body(): pl.pallas_call(functools.partial(kernel, nz), out_shape=(jax.ShapeDtypeSt...  85.8 us
    unnamed x17, local copies, waits for them, and re-layouts  8.48 us

profile of v1, /device:TPU:1, one launch (start us, length us, event | category | flops | bytes accessed | tf_op | source)
XLA Modules:
  0.0 94.9 jit_solution(6186631791330944213)
XLA Ops:
  0.6 0.0 copy-start
  0.6 1.9 %copy-done = bf16[4,6,512,128]{3,2,1,0:T(8,128)(2,1)S(1)} copy-done((bf16[4,6,512,128]{3,2,1,0:T(8,128)(2,1)S(1)}, bf16[4,6,512,128]{3,2,1,0:T(8,128)(2,1)}, u32[]{:S(2)}) %copy-start) | copy-done | bytes 3145752
  2.5 0.0 copy-start.1
  2.5 1.0 %copy-done.1 = bf16[4,512,128]{2,1,0:T(8,128)(2,1)S(1)} copy-done((bf16[4,512,128]{2,1,0:T(8,128)(2,1)S(1)}, bf16[4,512,128]{2,1,0:T(8,128)(2,1)}, u32[]{:S(2)}) %copy-start.1) | copy-done | bytes 524312
  3.6 0.0 copy-start.2
  3.6 0.9 copy-done.2
  4.5 0.0 copy-start.3
  4.5 0.7 copy-done.3
  5.2 0.0 copy-start.4
  5.2 0.7 copy-done.4
  5.8 0.0 copy-start.5
  5.8 0.7 copy-done.5
  6.5 0.0 copy-start.6
  6.5 0.7 copy-done.6
  7.2 85.8 %galerkin.1 = (bf16[4,128,128]{2,1,0:T(8,128)(2,1)S(1)}, f32[2,32,128]{2,1,0:T(8,128)S(1)}, f32[8,32,128]{2,1,0:T(8,128)S(1)}) custom-call(s32[4,6]{1,0:T(4,128)S(1)} %copy-done.3, s32[512]{0:T(512)S(1)} %copy-done.4, s32[256]{0:T(256)S(1)} %copy-done.6, f32[4,128]{1,0:T(4,128)S(1)} %copy-done.5, bf16[4,512,128]{2,1,0:T(8,128)(2,1)S(1)} %copy-done.1, ...), custom_call_target="tpu_custom_call" | custom-call | tf_op jit(solution)/shard_map/galerkin/pallas_call | solution.py:579
  93.0 0.7 copy.13
  93.6 0.6 copy.14
  94.3 0.7 copy.15
Async XLA Ops:
  0.6 1.9 %copy-start = (bf16[4,6,512,128]{3,2,1,0:T(8,128)(2,1)S(1)}, bf16[4,6,512,128]{3,2,1,0:T(8,128)(2,1)}, u32[]{:S(2)}) copy-start(bf16[4,6,512,128]{3,2,1,0:T(8,128)(2,1)} %nbrs_hbm.1) | copy-start | bytes 9437188
  2.5 1.0 %copy-start.1 = (bf16[4,512,128]{2,1,0:T(8,128)(2,1)S(1)}, bf16[4,512,128]{2,1,0:T(8,128)(2,1)}, u32[]{:S(2)}) copy-start(bf16[4,512,128]{2,1,0:T(8,128)(2,1)} %diag_hbm.1) | copy-start | bytes 1572868
  3.6 0.9 copy-start.2
  4.5 0.7 copy-start.3
  5.2 0.7 copy-start.4
  5.8 0.7 copy-start.5
  6.5 0.7 copy-start.6

commit v2 on v1

v2 whole, which is shorter than its diff:
```python
import functools

import jax
import jax.numpy as jnp
from jax import lax
from jax.experimental import pallas as pl
from jax.experimental.pallas import tpu as pltpu
from jax.sharding import PartitionSpec as P

MESH = pl.DeviceIdType.MESH
F32 = jnp.float32
BF16 = jnp.bfloat16
NL = 4
NBR = 6
BLK = 4
NX = 4
NC = 128
RB = 128
ROWS = RB * BLK
KK = (NBR + 1) * RB
HR = NC // BLK
SWEEPS = 2
LIMIT = 62 * 1024 * 1024


def remote(src, dst, send_sem, recv_sem, device):
    return pltpu.make_async_remote_copy(
        src_ref=src,
        dst_ref=dst,
        send_sem=send_sem,
        recv_sem=recv_sem,
        device_id=device,
        device_id_type=MESH,
    )


def kernel(
    nz,
    nbr_h,
    agg_h,
    grp_h,
    damp_h,
    diag_hbm,
    nbrs_hbm,
    bases_hbm,
    smooth_ref,
    coarse_ref,
    last_ref,
    nbr_s,
    agg_s,
    grp_s,
    damp_v,
    a_v,
    xe0,
    xe1,
    xe2,
    xg,
    xg2,
    dmp,
    ysum,
    y_out0,
    y_out1,
    y_in0,
    y_in1,
    xt,
    xa,
    zs,
    h_out,
    h_in,
    g_out,
    g_in,
    gx,
    c8h,
    hs,
    hx,
    km,
    pb,
    rz,
    rfar,
    four,
    l1,
    l2,
    ll,
    s_sem,
    a_sem,
    up_sem,
    down_sem,
    halo0_ss,
    halo0_rs,
    halo_ss,
    halo_rs,
    y_ss,
    y_rs,
    ag_ss,
    ag_rs,
    gh_ss,
    gh_rs,
    d_ss,
    d_rs,
    x_ss,
    x_rs,
    z_ss,
    z_rs,
    l1_ss,
    l1_rs,
    l2_ss,
    l2_rs,
    f_ss,
    f_rs,
):
    xe = (xe0, xe1, xe2)
    y_out = (y_out0, y_out1)
    y_in = (y_in0, y_in1)
    ne = nz * NX * 2
    zl_n = min(4, nz)
    zh_n = nz // zl_n
    me = lax.axis_index("elem")
    b = lax.axis_index("blk")
    core = lax.rem(me, 2)
    zc = lax.rem(me // 2, nz)
    xc = me // (2 * nz)
    rt = lax.rem(b + 1, BLK)
    op = lax.rem(b + 2, BLK)
    lt = lax.rem(b + 3, BLK)
    nxt = (lax.rem(me + 1, ne), b)
    prv = (lax.rem(me + ne - 1, ne), b)
    right, left, across = (me, rt), (me, lt), (me, op)

    def at(x, z, c):
        return ((x * nz + z) * 2 + c, b)

    above = at(xc, lax.rem(zc + 1, nz), core)
    below = at(xc, lax.rem(zc + nz - 1, nz), core)
    line = []
    for dx in range(NX):
        for dc in range(2):
            if dx or dc:
                line.append(at(lax.rem(xc + dx, NX), zc, lax.rem(core + dc, 2)))

    drains = []

    def finish():
        for drain in drains:
            drain()
        drains.clear()

    own_in = pltpu.make_async_copy(bases_hbm, xe[0].at[pl.ds(NL, NL)], s_sem.at[0])
    own_in.start()

    barrier = pltpu.get_barrier_semaphore()
    partners = [across, nxt, prv, right, left, above, below, *line]
    for dev in partners:
        pl.semaphore_signal(barrier, inc=1, device_id=dev, device_id_type=MESH)
    small = [
        pltpu.make_async_copy(src, dst, s_sem.at[i + 1])
        for i, (src, dst) in enumerate(
            ((damp_h, damp_v), (nbr_h, nbr_s), (agg_h, agg_s), (grp_h, grp_s))
        )
    ]
    for copy in small:
        copy.start()
    own_in.wait()
    pl.semaphore_wait(barrier, len(partners))

    h0n = remote(xe[0].at[pl.ds(NL, NL)], xe[0].at[pl.ds(0, NL)], halo0_ss.at[0], halo0_rs.at[0], nxt)
    h0p = remote(
        xe[0].at[pl.ds(NL, NL)], xe[0].at[pl.ds(2 * NL, NL)], halo0_ss.at[1], halo0_rs.at[1], prv
    )
    h0n.start()
    h0p.start()
    drains.append(h0n.wait_send)
    drains.append(h0p.wait_send)

    def load_a(e, carry):
        pltpu.make_async_copy(
            diag_hbm.at[e], a_v.at[e, :, pl.ds(0, RB)], a_sem.at[e]
        ).start()
        for k in range(NBR):
            pltpu.make_async_copy(
                nbrs_hbm.at[e, k],
                a_v.at[e, :, pl.ds((k + 1) * RB, RB)],
                a_sem.at[e],
            ).start()
        return carry

    lax.fori_loop(0, NL, load_a, 0)

    last_news = nz // 2 - 1
    news = [0]

    def pass_on():
        j = news[0]
        news[0] += 1
        if 1 <= j <= last_news:
            pl.semaphore_wait(up_sem, 1)
            pl.semaphore_wait(down_sem, 1)
        if j < last_news:
            pl.semaphore_signal(up_sem, inc=1, device_id=above, device_id_type=MESH)
            pl.semaphore_signal(down_sem, inc=1, device_id=below, device_id_type=MESH)

    for copy in small:
        copy.wait()
    for e in range(NL):
        dmp[e] = jnp.broadcast_to(damp_v[pl.ds(e, 1), :], (RB, NC)).T

    lane = lax.broadcasted_iota(jnp.int32, (16, 512), 1)
    row = lax.broadcasted_iota(jnp.int32, (16, 512), 0)

    def place(i, slots):
        xx, cc, j = i // 8, lax.rem(i // 4, 2), lax.rem(i, 4)
        a = agg_s[((xx * nz + zc) * 2 + cc) * NL + j]
        dev = a // 2
        mine = (lax.rem(dev, 2) == core) & (dev // (2 * nz) == xc)
        slot = jnp.where(mine, lax.rem(dev // 2, nz) * 2 + lax.rem(a, 2), -1)
        return jnp.where(lane // 16 == i, slot, slots)

    slots = lax.fori_loop(0, 32, place, jnp.full((16, 512), -1, jnp.int32))
    same_row = row == lax.rem(lane, 16)

    def fill(s, carry):
        km[pl.ds(pl.multiple_of(s * 16, 16), 16), :] = jnp.where(
            (slots == s) & same_row, 1.0, 0.0
        ).astype(BF16)
        return carry

    lax.fori_loop(0, 2 * nz, fill, 0)

    h0n.wait_recv()
    h0p.wait_recv()
    pass_on()

    first = (me - 1) * NL

    def nearby(e, k):
        return jnp.clip(nbr_s[e, k] - first, 0, 3 * NL - 1)

    def wait_a(e):
        pltpu.make_async_copy(a_v.at[e], a_v.at[e], a_sem.at[e]).wait()

    def y_copy(s, kind, e, dev):
        return remote(y_out[s].at[kind, e], y_in[s].at[kind, e], y_ss.at[s, kind, e], y_rs.at[s, kind, e], dev)

    def halo_next(st, e):
        return remote(
            xe[st].at[NL + e], xe[st].at[e], halo_ss.at[st - 1, 0, e], halo_rs.at[st - 1, 0, e], nxt
        )

    def halo_prev(st, e):
        return remote(
            xe[st].at[NL + e],
            xe[st].at[2 * NL + e],
            halo_ss.at[st - 1, 1, e],
            halo_rs.at[st - 1, 1, e],
            prv,
        )

    def sides(to_right):
        return (right, rt, left, lt) if to_right else (left, lt, right, rt)

    def pairs(step):
        def one(i, carry):
            step(i, True)
            step(i + 2, False)
            return carry

        lax.fori_loop(0, 2, one, 0)

    def gather_right(e, owner):
        return remote(
            xt.at[e], xa.at[e, owner], ag_ss.at[0, e], ag_rs.at[0, e], right
        )

    def gather_left(e, owner):
        return remote(
            xt.at[e], xa.at[e, owner], ag_ss.at[1, e], ag_rs.at[1, e], left
        )

    def gather_on(e, to_right, owner):
        near = sides(to_right)[0]
        return remote(xa.at[e, owner], xa.at[e, owner], ag_ss.at[2, e], ag_rs.at[2, e], near)

    def near_of(i):
        return lax.rem(b + 1 + 2 * i, BLK)

    for s in range(SWEEPS):

        def product(e, s=s):
            if s == 0:
                wait_a(e)
            xg[pl.ds(0, RB), :] = xe[s][NL + e]
            for k in range(NBR):
                xg[pl.ds((k + 1) * RB, RB), :] = xe[s][nearby(e, k)]
            y = jnp.dot(a_v[e], xg[...], preferred_element_type=F32)
            ysum[e] = y.reshape(BLK, RB, NC)

        def send_relayed(i, carry, s=s):
            product(i)
            near, far = near_of(i), near_of(i + 1)
            y_out[s][2, i] = ysum[i, op].astype(BF16)
            y_copy(s, 2, i, (me, near)).start()
            y_out[s][1 - i, i] = ysum[i, far].astype(BF16)
            y_copy(s, 1 - i, i, (me, far)).start()
            return carry

        def send_direct(e, carry, s=s):
            product(e)
            for kind, to in ((2, op), (0, rt), (1, lt)):
                y_out[s][kind, e] = ysum[e, to].astype(BF16)
                y_copy(s, kind, e, (me, to)).start()
            return carry

        def relay(i, carry, s=s):
            near = near_of(i)
            y_copy(s, 2, i, (me, near)).wait_recv()
            y_out[s][i, i] = (ysum[i, near] + y_in[s][2, i].astype(F32)).astype(BF16)
            y_copy(s, i, i, (me, near)).start()
            return carry

        lax.fori_loop(0, 2, send_relayed, 0)
        lax.fori_loop(2, NL, send_direct, 0)
        pass_on()
        lax.fori_loop(0, 2, relay, 0)

        def y_sent(e, carry, s=s):
            for kind in range(3):
                y_copy(s, kind, e, right).wait_send()
            return carry

        drains.append(functools.partial(lax.fori_loop, 0, NL, y_sent, 0))

        def update(e, direct, s=s):
            for kind in (0, 1, 2)[: 3 if direct else 2]:
                y_copy(s, kind, e, right).wait_recv()
            y = ysum[e, b] + y_in[s][0, e].astype(F32) + y_in[s][1, e].astype(F32)
            if direct:
                y = y + y_in[s][2, e].astype(F32)
            new = (xe[s][NL + e].astype(F32) - dmp[e] * y).astype(BF16)
            xe[s + 1][NL + e] = new
            halo_next(s + 1, e).start()
            halo_prev(s + 1, e).start()
            if s == SWEEPS - 1:
                turned = new.astype(F32).T.astype(BF16)
                xt[e] = turned
                gather_right(e, b).start()
                gather_left(e, b).start()
                smooth_ref[e] = new
                xa[e, b] = turned

        def update_relayed(e, carry, update=update):
            update(e, False)
            return carry

        def update_direct(e, carry, update=update):
            update(e, True)
            return carry

        lax.fori_loop(2, NL, update_direct, 0)
        lax.fori_loop(0, 2, update_relayed, 0)
        pass_on()

        def halo_in(e, carry, s=s):
            halo_next(s + 1, e).wait_recv()
            halo_prev(s + 1, e).wait_recv()
            return carry

        lax.fori_loop(0, NL, halo_in, 0)

        def halo_out(e, carry, s=s):
            halo_next(s + 1, e).wait_send()
            halo_prev(s + 1, e).wait_send()
            if s == SWEEPS - 1:
                gather_right(e, b).wait_send()
                gather_left(e, b).wait_send()
            return carry

        drains.append(functools.partial(lax.fori_loop, 0, NL, halo_out, 0))
        pass_on()
    def forward(e, to_right):
        if to_right:
            gather_right(e, lt).wait_recv()
            gather_on(e, True, lt).start()
        else:
            gather_left(e, rt).wait_recv()
            gather_on(e, False, rt).start()

    pairs(forward)
    drains.append(
        lambda: pairs(lambda e, to_right: gather_on(e, to_right, lt if to_right else rt).wait_send())
    )

    def couple(e, carry):
        own = me * NL + e
        own_agg = agg_s[own]
        own_grp = grp_s[own_agg]
        x_own = xe[SWEEPS][NL + e]
        xg2[pl.ds(0, RB), pl.ds(0, NC)] = x_own
        xg2[pl.ds(0, RB), pl.ds(NC, NC)] = x_own
        for k in range(NBR):
            near_agg = agg_s[nbr_s[e, k]]
            near_grp = grp_s[near_agg]
            x_near = xe[SWEEPS][nearby(e, k)].astype(F32)
            in_agg = jnp.where(near_agg == own_agg, 1.0, 0.0).astype(F32)
            in_grp = jnp.where(near_grp == own_grp, 1.0, 0.0).astype(F32)
            xg2[pl.ds((k + 1) * RB, RB), pl.ds(0, NC)] = (x_near * in_agg).astype(BF16)
            xg2[pl.ds((k + 1) * RB, RB), pl.ds(NC, NC)] = (x_near * in_grp).astype(BF16)
        zs[e] = jnp.dot(a_v[e], xg2[...], preferred_element_type=F32).astype(BF16)
        return carry

    lax.fori_loop(0, NL, couple, 0)
    pass_on()

    def contract(e, to_right):
        if to_right:
            gather_left(e, rt).wait_recv()
        else:
            gather_right(e, lt).wait_recv()
        gather_on(e, to_right, op).wait_recv()
        rows = jnp.concatenate([xa[e, r] for r in range(BLK)], axis=1)
        both = jnp.dot(rows, zs[e], preferred_element_type=F32)
        both = both.astype(BF16).reshape(BLK, HR, 2 * NC)
        g_out[:, e] = both[:, :, :NC]
        h_out[:, e] = both[:, :, NC:]

    pairs(contract)

    def gh_copy(which, kind, to):
        out, into = ((h_out, h_in), (g_out, g_in))[which]
        return remote(
            out.at[to], into.at[kind], gh_ss.at[which, kind], gh_rs.at[which, kind], (me, to)
        )

    for which in range(2):
        for kind, to in ((2, op), (0, rt), (1, lt)):
            gh_copy(which, kind, to).start()
            drains.append(gh_copy(which, kind, to).wait_send)

    def gh_sum(which):
        out, into = ((h_out, h_in), (g_out, g_in))[which]
        acc = out[b].astype(F32)
        for kind in range(3):
            gh_copy(which, kind, rt).wait_recv()
            acc = acc + into[kind].astype(F32)
        return acc.astype(BF16)

    mate = at(xc, zc, 1 - core)
    here = pl.ds(core * NL, NL)
    there = pl.ds((1 - core) * NL, NL)

    def mate_h(span):
        return remote(c8h.at[span], c8h.at[span], d_ss.at[0], d_rs.at[0], mate)

    def mate_g(span):
        return remote(gx.at[xc, span], gx.at[xc, span], d_ss.at[1], d_rs.at[1], mate)

    c8h[here] = gh_sum(0)
    mate_h(here).start()
    drains.append(mate_h(here).wait_send)
    gx[xc, here] = gh_sum(1)
    mate_g(here).start()
    drains.append(mate_g(here).wait_send)
    def x_g(dx, owner):
        dev = at(lax.rem(xc + dx, NX), zc, core)
        return remote(gx.at[owner], gx.at[owner], x_ss.at[dx - 1, 0], x_rs.at[dx - 1, 0], dev)

    def x_h(dx, owner):
        to = lax.rem(xc + dx, NX)
        return remote(
            hs.at[to], hx.at[owner], x_ss.at[dx - 1, 1], x_rs.at[dx - 1, 1], at(to, zc, core)
        )

    groups = [grp_s[agg_s[(me // 2) * (2 * NL) + i]] for i in range(2 * NL)]
    mate_h(there).wait_recv()
    for dx in (2, 1, 3, 0):
        to = lax.rem(xc + dx, NX)
        acc = jnp.zeros((HR, NC), F32)
        for i in range(2 * NL):
            acc = acc + jnp.where(groups[i] == 2 * to + core, 1.0, 0.0).astype(F32) * c8h[i].astype(
                F32
            )
        if dx:
            hs[to] = acc.astype(BF16)
            x_h(dx, xc).start()
            drains.append(x_h(dx, xc).wait_send)
        else:
            hx[xc] = acc.astype(BF16)
    mate_g(there).wait_recv()
    for dx in (2, 1, 3):
        x_g(dx, xc).start()
        drains.append(x_g(dx, xc).wait_send)

    zh, zl = zc // zl_n, lax.rem(zc, zl_n)

    def l1_copy(d, owner):
        dev = at(xc, zh * zl_n + lax.rem(zl + d, zl_n), core)
        return remote(l1.at[owner], l1.at[owner], l1_ss.at[d - 1], l1_rs.at[d - 1], dev)

    def l2_copy(d, owner):
        dev = at(xc, lax.rem(zh + d, zh_n) * zl_n + zl, core)
        return remote(l2.at[owner], l2.at[owner], l2_ss.at[d - 1], l2_rs.at[d - 1], dev)

    def summed(ref, n):
        acc = ref[0].astype(F32)
        for i in range(1, n):
            acc = acc + ref[i].astype(F32)
        return acc

    for dx in range(1, NX):
        x_h(dx, lax.rem(xc + NX - dx, NX)).wait_recv()
    l1[zl] = summed(hx, NX).astype(BF16)
    for d in range(1, zl_n):
        l1_copy(d, zl).start()
        drains.append(l1_copy(d, zl).wait_send)

    for dx in range(1, NX):
        x_g(dx, lax.rem(xc + NX - dx, NX)).wait_recv()
    for h in range(HR // 16):
        part = gx[:, :, h * 16 : (h + 1) * 16, :].reshape(512, NC)
        sums = jnp.dot(km[...], part, preferred_element_type=F32)
        pb[:, h * 16 : (h + 1) * 16, :] = sums.reshape(2 * nz, 16, NC).astype(BF16)

    def chunk(d):
        return pb.at[pl.ds(lax.rem(zc + nz + d, nz) * 2, 2)]

    def place_z(d):
        return at(xc, lax.rem(zc + nz + d, nz), core)

    eight = (1 - 2 * core) * 4

    def z_far(side, k):
        i = side * 3 + k - 1
        d = (1 - 2 * side) * k
        return remote(
            chunk((1 - 2 * side) * (k + 4)), rfar.at[side, k - 1], z_ss.at[i], z_rs.at[i], place_z(d)
        )

    def z_eight():
        return remote(chunk(8), rz.at[6], z_ss.at[6], z_rs.at[6], place_z(eight))

    def z_near(side, k):
        i = side * 3 + k - 1
        d = (1 - 2 * side) * k
        return remote(chunk(d), rz.at[i], z_ss.at[7 + i], z_rs.at[7 + i], place_z(d))

    def z_last(side):
        d = (1 - 2 * side) * 4
        return remote(four.at[side], rz.at[7 + side], z_ss.at[13 + side], z_rs.at[13 + side], place_z(d))

    z_eight().start()
    drains.append(z_eight().wait_send)
    for k in (3, 2, 1):
        for side in range(2):
            z_far(side, k).start()
            drains.append(z_far(side, k).wait_send)
    for k in (3, 2, 1):
        for side in range(2):
            z_near(side, k).start()
            drains.append(z_near(side, k).wait_send)

    for d in range(1, zl_n):
        l1_copy(d, lax.rem(zl + zl_n - d, zl_n)).wait_recv()
    l2[zh] = summed(l1, zl_n).astype(BF16)
    for d in range(1, zh_n):
        l2_copy(d, zh).start()
    sums = [chunk(4 - 8 * side)[...].astype(F32) for side in range(2)]
    for side in range(2):
        for k in (1, 2, 3):
            z_far(side, k).wait_recv()
            sums[side] = sums[side] + rfar[side, k - 1].astype(F32)
    z_eight().wait_recv()
    passed = rz[6].astype(F32)
    for side in range(2):
        share = jnp.where(core == side, 1.0, 0.0).astype(F32)
        four[side] = (sums[side] + share * passed).astype(BF16)
        z_last(side).start()
    finish()
    for d in range(1, zh_n):
        l2_copy(d, lax.rem(zh + zh_n - d, zh_n)).wait_recv()
    mine = 2 * xc + core
    ll[mine] = summed(l2, zh_n)

    def final_copy(i, owner):
        return remote(ll.at[owner], ll.at[owner], f_ss.at[i], f_rs.at[i], line[i])

    for i in range(len(line)):
        final_copy(i, mine).start()

    total = pb[pl.ds(zc * 2, 2)].astype(F32)
    for side in range(2):
        for k in (1, 2, 3):
            z_near(side, k).wait_recv()
            total = total + rz[side * 3 + k - 1].astype(F32)
    for side in range(2):
        z_last(side).wait_recv()
        total = total + rz[7 + side].astype(F32)
    coarse_ref[...] = total
    for side in range(2):
        z_last(side).wait_send()
    for d in range(1, zh_n):
        l2_copy(d, zh).wait_send()

    i = 0
    for dx in range(NX):
        for dc in range(2):
            if dx or dc:
                owner = 2 * lax.rem(xc + NX - dx, NX) + lax.rem(core + dc, 2)
                final_copy(i, owner).wait_recv()
                i += 1
    last_ref[...] = ll[...]
    for i in range(len(line)):
        final_copy(i, mine).wait_send()


def write_out(a, b, c, a_out, b_out, c_out, a_v, b_v, c_v, in_sem, out_sem):
    held = ((a, a_v, a_out), (b, b_v, b_out), (c, c_v, c_out))
    reads = [pltpu.make_async_copy(x, v, in_sem.at[i]) for i, (x, v, _) in enumerate(held)]
    writes = [pltpu.make_async_copy(v, o, out_sem.at[i]) for i, (_, v, o) in enumerate(held)]
    for read in reads:
        read.start()
    for read, write in zip(reads, writes):
        read.wait()
        write.start()
    for write in writes:
        write.wait()


def body(nz, diag, nbrs, neighbours, damping, bases, agglomerate, group):
    vmem = pl.BlockSpec(memory_space=pltpu.VMEM)
    hbm = pl.BlockSpec(memory_space=pltpu.HBM)
    zl_n = min(4, nz)
    dma = pltpu.SemaphoreType.DMA
    regular = pltpu.SemaphoreType.REGULAR
    V = pltpu.VMEM
    scratch = [
        pltpu.SMEM((NL, NBR), jnp.int32),
        pltpu.SMEM(agglomerate.shape, jnp.int32),
        pltpu.SMEM(group.shape, jnp.int32),
        V((NL, RB), F32),
        V((NL, ROWS, KK), BF16),
        *[V((3 * NL, RB, NC), BF16) for _ in range(SWEEPS + 1)],
        V((KK, NC), BF16),
        V((KK, 2 * NC), BF16),
        V((NL, RB, NC), F32),
        V((NL, BLK, RB, NC), F32),
        *[V((3, NL, RB, NC), BF16) for _ in range(4)],
        V((NL, RB, NC), BF16),
        V((NL, BLK, RB, NC), BF16),
        V((NL, ROWS, 2 * NC), BF16),
        V((BLK, NL, HR, NC), BF16),
        V((3, NL, HR, NC), BF16),
        V((BLK, NL, HR, NC), BF16),
        V((3, NL, HR, NC), BF16),
        V((NX, 2 * NL, HR, NC), BF16),
        V((2 * NL, HR, NC), BF16),
        V((NX, HR, NC), BF16),
        V((NX, HR, NC), BF16),
        V((2 * nz * 16, 512), BF16),
        V((2 * nz, HR, NC), BF16),
        V((9, 2, HR, NC), BF16),
        V((2, 3, 2, HR, NC), BF16),
        V((2, 2, HR, NC), BF16),
        V((zl_n, HR, NC), BF16),
        V((nz // zl_n, HR, NC), BF16),
        V((8, HR, NC), F32),
        dma((5,)),
        dma((NL,)),
        regular,
        regular,
        dma((2,)),
        dma((2,)),
        dma((SWEEPS, 2, NL)),
        dma((SWEEPS, 2, NL)),
        dma((SWEEPS, 3, NL)),
        dma((SWEEPS, 3, NL)),
        dma((3, NL)),
        dma((3, NL)),
        dma((2, 3)),
        dma((2, 3)),
        dma((2,)),
        dma((2,)),
        dma((NX - 1, 2)),
        dma((NX - 1, 2)),
        dma((nz - 1,)),
        dma((nz - 1,)),
        dma((3,)),
        dma((3,)),
        dma((3,)),
        dma((3,)),
        dma((2 * NX - 1,)),
        dma((2 * NX - 1,)),
    ]
    out = pl.pallas_call(
        functools.partial(kernel, nz),
        out_shape=(
            jax.ShapeDtypeStruct((NL, RB, NC), BF16),
            jax.ShapeDtypeStruct((2, HR, NC), F32),
            jax.ShapeDtypeStruct((8, HR, NC), F32),
        ),
        in_specs=[hbm] * 7,
        out_specs=(vmem, vmem, vmem),
        scratch_shapes=scratch,
        compiler_params=pltpu.CompilerParams(
            collective_id=0, has_side_effects=True, vmem_limit_bytes=LIMIT
        ),
        name="galerkin",
    )(neighbours, agglomerate, group, damping, diag, nbrs, bases)
    return pl.pallas_call(
        write_out,
        out_shape=tuple(jax.ShapeDtypeStruct(o.shape, o.dtype) for o in out),
        in_specs=[hbm] * 3,
        out_specs=(hbm,) * 3,
        scratch_shapes=[*[V(o.shape, o.dtype) for o in out], dma((3,)), dma((3,))],
        compiler_params=pltpu.CompilerParams(vmem_limit_bytes=LIMIT),
        name="write_out",
    )(*out)


def solution(mesh):
    nz = mesh.shape["elem"] // (2 * NX)
    return jax.shard_map(
        functools.partial(body, nz),
        mesh=mesh,
        in_specs=(
            P("elem", None, "blk"),
            P("elem", None, None, "blk"),
            P("elem", None),
            P("elem", "blk"),
            P("elem", "blk", None),
            P(),
            P(),
        ),
        out_specs=(P("elem", "blk", None), P("elem", "blk", None), P(None, "blk", None)),
        check_vma=False,
    )
```

time: 95.2 us -> 77.6 us (0.82)
  Pallas kernels: 85.8 us -> 76.8 us
  local copies, waits for them, and re-layouts: 8.48 us -> 0 us
    pallas_call x1, Pallas kernels: 85.8 us -> 75.1 us  [body(): pl.pallas_call(functools.partial(kernel, nz), out_shape=(jax.ShapeDtypeSt...]
    unnamed x17 -> x0, local copies, waits for them, and re-layouts: 8.48 us -> none
    pallas_call x0 -> x1, Pallas kernels: none -> 1.69 us  [body(): pl.pallas_call(write_out, out_shape=tuple((jax.ShapeDtypeStruct(o.shape,...]
where the time goes in v2:
time: 77.6 us; the launch traced here: 77.5 us
  Pallas kernels  76.8 us (99%)
    pallas_call x1, Pallas kernels, body(): pl.pallas_call(functools.partial(kernel, nz), out_shape=(jax.ShapeDtypeSt...  75.1 us
    pallas_call x1, Pallas kernels, body(): pl.pallas_call(write_out, out_shape=tuple((jax.ShapeDtypeStruct(o.shape,...  1.69 us

profile of v2, /device:TPU:1, one launch (start us, length us, event | category | flops | bytes accessed | tf_op | source)
XLA Modules:
  0.0 77.5 jit_solution(16325609620203315139)
XLA Ops:
  0.6 75.1 %galerkin.1 = (bf16[4,128,128]{2,1,0:T(8,128)(2,1)}, f32[2,32,128]{2,1,0:T(8,128)}, f32[8,32,128]{2,1,0:T(8,128)}) custom-call(s32[4,6]{1,0:T(4,128)} %nbr_h.1, s32[512]{0:T(512)} %agg_h.1, s32[256]{0:T(256)} %grp_h.1, f32[4,128]{1,0:T(4,128)} %damp_h.1, bf16[4,512,128]{2,1,0:T(8,128)(2,1)} %diag_hbm.1, bf16[4,6,512,128]{3,2,1,0:T(8,128)(2,1)} %nbrs_hbm.1, ...), custom_call_target="tpu_custom_call" | custom-call | tf_op jit(solution)/shard_map/galerkin/pallas_call | solution.py:691
  75.8 1.7 %write_out.1 = (bf16[4,128,128]{2,1,0:T(8,128)(2,1)}, f32[2,32,128]{2,1,0:T(8,128)}, f32[8,32,128]{2,1,0:T(8,128)}) custom-call(bf16[4,128,128]{2,1,0:T(8,128)(2,1)} %get-tuple-element.6.a, f32[2,32,128]{2,1,0:T(8,128)} %get-tuple-element.7.b, f32[8,32,128]{2,1,0:T(8,128)} %get-tuple-element.8.c), custom_call_target="tpu_custom_call" | custom-call | tf_op jit(solution)/shard_map/write_out/pallas_call | solution.py:706

commit v3 on v2

--- a/solution.py
+++ b/solution.py
@@ -65,13 +65,11 @@
     xt,
     xa,
     zs,
+    h_part,
     h_out,
-    h_in,
     g_out,
     g_in,
     gx,
-    c8h,
-    hs,
     hx,
     km,
     pb,
@@ -85,6 +83,7 @@
     a_sem,
     up_sem,
     down_sem,
+    side_sem,
     halo0_ss,
     halo0_rs,
     halo_ss,
@@ -93,10 +92,10 @@
     y_rs,
     ag_ss,
     ag_rs,
-    gh_ss,
-    gh_rs,
-    d_ss,
-    d_rs,
+    h_ss,
+    h_rs,
+    g_ss,
+    g_rs,
     x_ss,
     x_rs,
     z_ss,
@@ -168,6 +167,8 @@
     )
     h0n.start()
     h0p.start()
+    for dev in (right, left, across):
+        pl.semaphore_signal(side_sem, inc=1, device_id=dev, device_id_type=MESH)
     drains.append(h0n.wait_send)
     drains.append(h0p.wait_send)
 
@@ -417,77 +418,69 @@
         gather_on(e, to_right, op).wait_recv()
         rows = jnp.concatenate([xa[e, r] for r in range(BLK)], axis=1)
         both = jnp.dot(rows, zs[e], preferred_element_type=F32)
-        both = both.astype(BF16).reshape(BLK, HR, 2 * NC)
-        g_out[:, e] = both[:, :, :NC]
-        h_out[:, e] = both[:, :, NC:]
+        g_out[:, e] = both[:, :NC].astype(BF16).reshape(BLK, HR, NC)
+        h_part[e] = both[:, NC:]
 
     pairs(contract)
 
-    def gh_copy(which, kind, to):
-        out, into = ((h_out, h_in), (g_out, g_in))[which]
-        return remote(
-            out.at[to], into.at[kind], gh_ss.at[which, kind], gh_rs.at[which, kind], (me, to)
-        )
-
-    for which in range(2):
-        for kind, to in ((2, op), (0, rt), (1, lt)):
-            gh_copy(which, kind, to).start()
-            drains.append(gh_copy(which, kind, to).wait_send)
-
-    def gh_sum(which):
-        out, into = ((h_out, h_in), (g_out, g_in))[which]
-        acc = out[b].astype(F32)
-        for kind in range(3):
-            gh_copy(which, kind, rt).wait_recv()
-            acc = acc + into[kind].astype(F32)
-        return acc.astype(BF16)
-
-    mate = at(xc, zc, 1 - core)
-    here = pl.ds(core * NL, NL)
-    there = pl.ds((1 - core) * NL, NL)
-
-    def mate_h(span):
-        return remote(c8h.at[span], c8h.at[span], d_ss.at[0], d_rs.at[0], mate)
-
-    def mate_g(span):
-        return remote(gx.at[xc, span], gx.at[xc, span], d_ss.at[1], d_rs.at[1], mate)
-
-    c8h[here] = gh_sum(0)
-    mate_h(here).start()
-    drains.append(mate_h(here).wait_send)
-    gx[xc, here] = gh_sum(1)
-    mate_g(here).start()
-    drains.append(mate_g(here).wait_send)
-    def x_g(dx, owner):
-        dev = at(lax.rem(xc + dx, NX), zc, core)
-        return remote(gx.at[owner], gx.at[owner], x_ss.at[dx - 1, 0], x_rs.at[dx - 1, 0], dev)
-
-    def x_h(dx, owner):
-        to = lax.rem(xc + dx, NX)
-        return remote(
-            hs.at[to], hx.at[owner], x_ss.at[dx - 1, 1], x_rs.at[dx - 1, 1], at(to, zc, core)
-        )
-
-    groups = [grp_s[agg_s[(me // 2) * (2 * NL) + i]] for i in range(2 * NL)]
-    mate_h(there).wait_recv()
-    for dx in (2, 1, 3, 0):
-        to = lax.rem(xc + dx, NX)
-        acc = jnp.zeros((HR, NC), F32)
-        for i in range(2 * NL):
-            acc = acc + jnp.where(groups[i] == 2 * to + core, 1.0, 0.0).astype(F32) * c8h[i].astype(
-                F32
-            )
-        if dx:
-            hs[to] = acc.astype(BF16)
-            x_h(dx, xc).start()
-            drains.append(x_h(dx, xc).wait_send)
-        else:
-            hx[xc] = acc.astype(BF16)
-    mate_g(there).wait_recv()
-    for dx in (2, 1, 3):
-        x_g(dx, xc).start()
-        drains.append(x_g(dx, xc).wait_send)
-
+    def g_copy(kind, to):
+        return remote(g_out.at[to], g_in.at[kind], g_ss.at[kind], g_rs.at[kind], (me, to))
+
+    for kind, to in ((2, op), (0, rt), (1, lt)):
+        g_copy(kind, to).start()
+        drains.append(g_copy(kind, to).wait_send)
+
+    groups = [grp_s[agg_s[me * NL + e]] for e in range(NL)]
+
+    def group_sum(g, carry):
+        acc = jnp.zeros((NC, NC), F32)
+        for e in range(NL):
+            acc = acc + jnp.where(groups[e] == g, 1.0, 0.0).astype(F32) * h_part[e]
+        h_out[g] = acc.astype(BF16).reshape(BLK, HR, NC)
+        return carry
+
+    lax.fori_loop(0, 2 * NX, group_sum, 0)
+    pl.semaphore_wait(side_sem, 3)
+
+    def h_copy(dx, dc, dy):
+        x, c, y = lax.rem(xc + dx, NX), lax.rem(core + dc, 2), lax.rem(b + dy, BLK)
+        i = (dx * 2 + dc) * BLK + dy - 1
+        dev = ((x * nz + zc) * 2 + c, y)
+        return remote(h_out.at[2 * x + c, y], hx.at[(2 * xc + core) * BLK + b], h_ss.at[i], h_rs.at[i], dev)
+
+    def h_arrival(dx, dc, dy):
+        x, c, y = lax.rem(xc + NX - dx, NX), lax.rem(core + dc, 2), lax.rem(b + BLK - dy, BLK)
+        i = (dx * 2 + dc) * BLK + dy - 1
+        return remote(h_out.at[0, 0], hx.at[(2 * x + c) * BLK + y], h_ss.at[i], h_rs.at[i], right)
+
+    others = [
+        (dx, dc, dy)
+        for dx in (2, 1, 3, 0)
+        for dy in (2, 1, 3, 0)
+        for dc in (1, 0)
+        if dx or dc or dy
+    ]
+    for o in others:
+        h_copy(*o).start()
+        drains.append(h_copy(*o).wait_send)
+    hx[(2 * xc + core) * BLK + b] = h_out[2 * xc + core, b]
+
+    acc = g_out[b].astype(F32)
+    for kind in (0, 1, 2):
+        g_copy(kind, rt).wait_recv()
+        acc = acc + g_in[kind].astype(F32)
+    gx[2 * xc + core] = acc.astype(BF16)
+
+    def x_g(i, owner):
+        return remote(gx.at[owner], gx.at[owner], x_ss.at[i], x_rs.at[i], line[i])
+
+    def line_owner(i):
+        k = i + 1
+        return 2 * lax.rem(xc + NX - k // 2, NX) + lax.rem(core + k % 2, 2)
+
+    for i in (3, 4, 1, 2, 5, 6, 0):
+        x_g(i, 2 * xc + core).start()
+        drains.append(x_g(i, 2 * xc + core).wait_send)
     zh, zl = zc // zl_n, lax.rem(zc, zl_n)
 
     def l1_copy(d, owner):
@@ -504,15 +497,15 @@
             acc = acc + ref[i].astype(F32)
         return acc
 
-    for dx in range(1, NX):
-        x_h(dx, lax.rem(xc + NX - dx, NX)).wait_recv()
-    l1[zl] = summed(hx, NX).astype(BF16)
+    for o in others:
+        h_arrival(*o).wait_recv()
+    l1[zl] = summed(hx, 2 * NX * BLK).astype(BF16)
     for d in range(1, zl_n):
         l1_copy(d, zl).start()
         drains.append(l1_copy(d, zl).wait_send)
 
-    for dx in range(1, NX):
-        x_g(dx, lax.rem(xc + NX - dx, NX)).wait_recv()
+    for i in range(len(line)):
+        x_g(i, line_owner(i)).wait_recv()
     for h in range(HR // 16):
         part = gx[:, :, h * 16 : (h + 1) * 16, :].reshape(512, NC)
         sums = jnp.dot(km[...], part, preferred_element_type=F32)
@@ -544,6 +537,12 @@
     def z_last(side):
         d = (1 - 2 * side) * 4
         return remote(four.at[side], rz.at[7 + side], z_ss.at[13 + side], z_rs.at[13 + side], place_z(d))
+
+    for d in range(1, zl_n):
+        l1_copy(d, lax.rem(zl + zl_n - d, zl_n)).wait_recv()
+    l2[zh] = summed(l1, zl_n).astype(BF16)
+    for d in range(1, zh_n):
+        l2_copy(d, zh).start()
 
     z_eight().start()
     drains.append(z_eight().wait_send)
@@ -556,11 +555,7 @@
             z_near(side, k).start()
             drains.append(z_near(side, k).wait_send)
 
-    for d in range(1, zl_n):
-        l1_copy(d, lax.rem(zl + zl_n - d, zl_n)).wait_recv()
-    l2[zh] = summed(l1, zl_n).astype(BF16)
-    for d in range(1, zh_n):
-        l2_copy(d, zh).start()
+    finish()
     sums = [chunk(4 - 8 * side)[...].astype(F32) for side in range(2)]
     for side in range(2):
         for k in (1, 2, 3):
@@ -572,11 +567,10 @@
         share = jnp.where(core == side, 1.0, 0.0).astype(F32)
         four[side] = (sums[side] + share * passed).astype(BF16)
         z_last(side).start()
-    finish()
     for d in range(1, zh_n):
         l2_copy(d, lax.rem(zh + zh_n - d, zh_n)).wait_recv()
     mine = 2 * xc + core
-    ll[mine] = summed(l2, zh_n)
+    ll[mine] = summed(l2, zh_n).astype(BF16)
 
     def final_copy(i, owner):
         return remote(ll.at[owner], ll.at[owner], f_ss.at[i], f_rs.at[i], line[i])
@@ -598,14 +592,9 @@
     for d in range(1, zh_n):
         l2_copy(d, zh).wait_send()
 
-    i = 0
-    for dx in range(NX):
-        for dc in range(2):
-            if dx or dc:
-                owner = 2 * lax.rem(xc + NX - dx, NX) + lax.rem(core + dc, 2)
-                final_copy(i, owner).wait_recv()
-                i += 1
-    last_ref[...] = ll[...]
+    for i in range(len(line)):
+        final_copy(i, line_owner(i)).wait_recv()
+    last_ref[...] = ll[...].astype(F32)
     for i in range(len(line)):
         final_copy(i, mine).wait_send()
 
@@ -645,14 +634,12 @@
         V((NL, RB, NC), BF16),
         V((NL, BLK, RB, NC), BF16),
         V((NL, ROWS, 2 * NC), BF16),
+        V((NL, NC, NC), F32),
+        V((2 * NX, BLK, HR, NC), BF16),
         V((BLK, NL, HR, NC), BF16),
         V((3, NL, HR, NC), BF16),
-        V((BLK, NL, HR, NC), BF16),
-        V((3, NL, HR, NC), BF16),
-        V((NX, 2 * NL, HR, NC), BF16),
-        V((2 * NL, HR, NC), BF16),
-        V((NX, HR, NC), BF16),
-        V((NX, HR, NC), BF16),
+        V((2 * NX, NL, HR, NC), BF16),
+        V((2 * NX * BLK, HR, NC), BF16),
         V((2 * nz * 16, 512), BF16),
         V((2 * nz, HR, NC), BF16),
         V((9, 2, HR, NC), BF16),
@@ -660,9 +647,10 @@
         V((2, 2, HR, NC), BF16),
         V((zl_n, HR, NC), BF16),
         V((nz // zl_n, HR, NC), BF16),
-        V((8, HR, NC), F32),
+        V((8, HR, NC), BF16),
         dma((5,)),
         dma((NL,)),
+        regular,
         regular,
         regular,
         dma((2,)),
@@ -673,12 +661,12 @@
         dma((SWEEPS, 3, NL)),
         dma((3, NL)),
         dma((3, NL)),
-        dma((2, 3)),
-        dma((2, 3)),
-        dma((2,)),
-        dma((2,)),
-        dma((NX - 1, 2)),
-        dma((NX - 1, 2)),
+        dma((2 * NX * BLK - 1,)),
+        dma((2 * NX * BLK - 1,)),
+        dma((3,)),
+        dma((3,)),
+        dma((2 * NX - 1,)),
+        dma((2 * NX - 1,)),
         dma((nz - 1,)),
         dma((nz - 1,)),
         dma((3,)),

time: 77.6 us -> 72.7 us (0.937)
  Pallas kernels: 76.8 us -> 71.9 us
    pallas_call x1, Pallas kernels: 75.1 us -> 70.2 us  [body(): pl.pallas_call(functools.partial(kernel, nz), out_shape=(jax.ShapeDtypeSt...]
where the time goes in v3:
time: 72.7 us; the launch traced here: 72.5 us
  Pallas kernels  71.9 us (99%)
    pallas_call x1, Pallas kernels, body(): pl.pallas_call(functools.partial(kernel, nz), out_shape=(jax.ShapeDtypeSt...  70.2 us
    pallas_call x1, Pallas kernels, body(): pl.pallas_call(write_out, out_shape=tuple((jax.ShapeDtypeStruct(o.shape,...  1.69 us

profile of v3, /device:TPU:1, one launch (start us, length us, event | category | flops | bytes accessed | tf_op | source)
XLA Modules:
  0.0 72.5 jit_solution(12093662334533437379)
XLA Ops:
  0.6 70.2 %galerkin.1 = (bf16[4,128,128]{2,1,0:T(8,128)(2,1)}, f32[2,32,128]{2,1,0:T(8,128)}, f32[8,32,128]{2,1,0:T(8,128)}) custom-call(s32[4,6]{1,0:T(4,128)} %nbr_h.1, s32[512]{0:T(512)} %agg_h.1, s32[256]{0:T(256)} %grp_h.1, f32[4,128]{1,0:T(4,128)} %damp_h.1, bf16[4,512,128]{2,1,0:T(8,128)(2,1)} %diag_hbm.1, bf16[4,6,512,128]{3,2,1,0:T(8,128)(2,1)} %nbrs_hbm.1, ...), custom_call_target="tpu_custom_call" | custom-call | tf_op jit(solution)/shard_map/galerkin/pallas_call | solution.py:679
  70.8 1.7 %write_out.1 = (bf16[4,128,128]{2,1,0:T(8,128)(2,1)}, f32[2,32,128]{2,1,0:T(8,128)}, f32[8,32,128]{2,1,0:T(8,128)}) custom-call(bf16[4,128,128]{2,1,0:T(8,128)(2,1)} %get-tuple-element.6.a, f32[2,32,128]{2,1,0:T(8,128)} %get-tuple-element.7.b, f32[8,32,128]{2,1,0:T(8,128)} %get-tuple-element.8.c), custom_call_target="tpu_custom_call" | custom-call | tf_op jit(solution)/shard_map/write_out/pallas_call | solution.py:694

commit v4 on v3

--- a/solution.py
+++ b/solution.py
@@ -258,14 +258,6 @@
     def sides(to_right):
         return (right, rt, left, lt) if to_right else (left, lt, right, rt)
 
-    def pairs(step):
-        def one(i, carry):
-            step(i, True)
-            step(i + 2, False)
-            return carry
-
-        lax.fori_loop(0, 2, one, 0)
-
     def gather_right(e, owner):
         return remote(
             xt.at[e], xa.at[e, owner], ag_ss.at[0, e], ag_rs.at[0, e], right
@@ -279,6 +271,9 @@
     def gather_on(e, to_right, owner):
         near = sides(to_right)[0]
         return remote(xa.at[e, owner], xa.at[e, owner], ag_ss.at[2, e], ag_rs.at[2, e], near)
+
+    def gather_across(e, owner):
+        return remote(xt.at[e], xa.at[e, owner], ag_ss.at[2, e], ag_rs.at[2, e], across)
 
     def near_of(i):
         return lax.rem(b + 1 + 2 * i, BLK)
@@ -344,6 +339,8 @@
                 xt[e] = turned
                 gather_right(e, b).start()
                 gather_left(e, b).start()
+                if not direct:
+                    gather_across(e, b).start()
                 smooth_ref[e] = new
                 xa[e, b] = turned
 
@@ -376,18 +373,14 @@
 
         drains.append(functools.partial(lax.fori_loop, 0, NL, halo_out, 0))
         pass_on()
-    def forward(e, to_right):
-        if to_right:
-            gather_right(e, lt).wait_recv()
-            gather_on(e, True, lt).start()
-        else:
-            gather_left(e, rt).wait_recv()
-            gather_on(e, False, rt).start()
-
-    pairs(forward)
-    drains.append(
-        lambda: pairs(lambda e, to_right: gather_on(e, to_right, lt if to_right else rt).wait_send())
-    )
+    gather_right(2, lt).wait_recv()
+    gather_on(2, True, lt).start()
+    gather_left(3, rt).wait_recv()
+    gather_on(3, False, rt).start()
+    for e in range(2):
+        drains.append(gather_across(e, b).wait_send)
+    drains.append(gather_on(2, True, lt).wait_send)
+    drains.append(gather_on(3, False, rt).wait_send)
 
     def couple(e, carry):
         own = me * NL + e
@@ -410,18 +403,20 @@
     lax.fori_loop(0, NL, couple, 0)
     pass_on()
 
-    def contract(e, to_right):
-        if to_right:
-            gather_left(e, rt).wait_recv()
-        else:
-            gather_right(e, lt).wait_recv()
-        gather_on(e, to_right, op).wait_recv()
+    def contract(e, carry):
+        gather_across(e, op).wait_recv()
         rows = jnp.concatenate([xa[e, r] for r in range(BLK)], axis=1)
         both = jnp.dot(rows, zs[e], preferred_element_type=F32)
         g_out[:, e] = both[:, :NC].astype(BF16).reshape(BLK, HR, NC)
         h_part[e] = both[:, NC:]
-
-    pairs(contract)
+        return carry
+
+    for e in range(NL):
+        if e != 3:
+            gather_left(e, rt).wait_recv()
+        if e != 2:
+            gather_right(e, lt).wait_recv()
+    lax.fori_loop(0, NL, contract, 0)
 
     def g_copy(kind, to):
         return remote(g_out.at[to], g_in.at[kind], g_ss.at[kind], g_rs.at[kind], (me, to))

time: 72.7 us -> 71.8 us (0.988)
  Pallas kernels: 71.9 us -> 70.9 us
    pallas_call x1, Pallas kernels: 70.2 us -> 69.2 us  [body(): pl.pallas_call(functools.partial(kernel, nz), out_shape=(jax.ShapeDtypeSt...]
where the time goes in v4:
time: 71.8 us; the launch traced here: 71.6 us
  Pallas kernels  70.9 us (99%)
    pallas_call x1, Pallas kernels, body(): pl.pallas_call(functools.partial(kernel, nz), out_shape=(jax.ShapeDtypeSt...  69.2 us
    pallas_call x1, Pallas kernels, body(): pl.pallas_call(write_out, out_shape=tuple((jax.ShapeDtypeStruct(o.shape,...  1.69 us

profile of v4, /device:TPU:1, one launch (start us, length us, event | category | flops | bytes accessed | tf_op | source)
XLA Modules:
  0.0 71.6 jit_solution(12273126861961530039)
XLA Ops:
  0.6 69.2 %galerkin.1 = (bf16[4,128,128]{2,1,0:T(8,128)(2,1)}, f32[2,32,128]{2,1,0:T(8,128)}, f32[8,32,128]{2,1,0:T(8,128)}) custom-call(s32[4,6]{1,0:T(4,128)} %nbr_h.1, s32[512]{0:T(512)} %agg_h.1, s32[256]{0:T(256)} %grp_h.1, f32[4,128]{1,0:T(4,128)} %damp_h.1, bf16[4,512,128]{2,1,0:T(8,128)(2,1)} %diag_hbm.1, bf16[4,6,512,128]{3,2,1,0:T(8,128)(2,1)} %nbrs_hbm.1, ...), custom_call_target="tpu_custom_call" | custom-call | tf_op jit(solution)/shard_map/galerkin/pallas_call | solution.py:674
  69.9 1.7 %write_out.1 = (bf16[4,128,128]{2,1,0:T(8,128)(2,1)}, f32[2,32,128]{2,1,0:T(8,128)}, f32[8,32,128]{2,1,0:T(8,128)}) custom-call(bf16[4,128,128]{2,1,0:T(8,128)(2,1)} %get-tuple-element.6.a, f32[2,32,128]{2,1,0:T(8,128)} %get-tuple-element.7.b, f32[8,32,128]{2,1,0:T(8,128)} %get-tuple-element.8.c), custom_call_target="tpu_custom_call" | custom-call | tf_op jit(solution)/shard_map/write_out/pallas_call | solution.py:689

commit v5 on v4

--- a/solution.py
+++ b/solution.py
@@ -499,6 +499,11 @@
         l1_copy(d, zl).start()
         drains.append(l1_copy(d, zl).wait_send)
 
+    for d in range(1, zl_n):
+        l1_copy(d, lax.rem(zl + zl_n - d, zl_n)).wait_recv()
+    l2[zh] = summed(l1, zl_n).astype(BF16)
+    for d in range(1, zh_n):
+        l2_copy(d, zh).start()
     for i in range(len(line)):
         x_g(i, line_owner(i)).wait_recv()
     for h in range(HR // 16):
@@ -533,11 +538,6 @@
         d = (1 - 2 * side) * 4
         return remote(four.at[side], rz.at[7 + side], z_ss.at[13 + side], z_rs.at[13 + side], place_z(d))
 
-    for d in range(1, zl_n):
-        l1_copy(d, lax.rem(zl + zl_n - d, zl_n)).wait_recv()
-    l2[zh] = summed(l1, zl_n).astype(BF16)
-    for d in range(1, zh_n):
-        l2_copy(d, zh).start()
 
     z_eight().start()
     drains.append(z_eight().wait_send)

time: 71.8 us -> 71.3 us (level)
  no operation moved by 1% of the time
where the time goes in v5:
time: 71.3 us; the launch traced here: 71.1 us
  Pallas kernels  70.5 us (99%)
    pallas_call x1, Pallas kernels, body(): pl.pallas_call(functools.partial(kernel, nz), out_shape=(jax.ShapeDtypeSt...  68.8 us
    pallas_call x1, Pallas kernels, body(): pl.pallas_call(write_out, out_shape=tuple((jax.ShapeDtypeStruct(o.shape,...  1.69 us

profile of v5, /device:TPU:1, one launch (start us, length us, event | category | flops | bytes accessed | tf_op | source)
XLA Modules:
  0.0 71.1 jit_solution(11406350585607571743)
XLA Ops:
  0.6 68.8 %galerkin.1 = (bf16[4,128,128]{2,1,0:T(8,128)(2,1)}, f32[2,32,128]{2,1,0:T(8,128)}, f32[8,32,128]{2,1,0:T(8,128)}) custom-call(s32[4,6]{1,0:T(4,128)} %nbr_h.1, s32[512]{0:T(512)} %agg_h.1, s32[256]{0:T(256)} %grp_h.1, f32[4,128]{1,0:T(4,128)} %damp_h.1, bf16[4,512,128]{2,1,0:T(8,128)(2,1)} %diag_hbm.1, bf16[4,6,512,128]{3,2,1,0:T(8,128)(2,1)} %nbrs_hbm.1, ...), custom_call_target="tpu_custom_call" | custom-call | tf_op jit(solution)/shard_map/galerkin/pallas_call | solution.py:674
  69.5 1.7 %write_out.1 = (bf16[4,128,128]{2,1,0:T(8,128)(2,1)}, f32[2,32,128]{2,1,0:T(8,128)}, f32[8,32,128]{2,1,0:T(8,128)}) custom-call(bf16[4,128,128]{2,1,0:T(8,128)(2,1)} %get-tuple-element.6.a, f32[2,32,128]{2,1,0:T(8,128)} %get-tuple-element.7.b, f32[8,32,128]{2,1,0:T(8,128)} %get-tuple-element.8.c), custom_call_target="tpu_custom_call" | custom-call | tf_op jit(solution)/shard_map/write_out/pallas_call | solution.py:689
